TPU v7x, 32 devices: a whole 2x2x4 slice. The times are simulated.
32 devices in a mesh: bead: 4 (over y, x), dom: 8 (over z, core).
Axes of the slice: x: 2, y: 2, z: 4, core: 2. Of those that a mesh axis runs over, the one named last changes fastest.
Arguments:
- mode_pos: float32 [16, 3, 6144], P('bead', None, 'dom'), may hold values from -6 to 6
- mode_vel: float32 [16, 3, 6144], P('bead', None, 'dom'), may hold values from -6 to 6
- charges: float32 [6144], P('dom'), may hold values from -1.5 to 1.5
Outputs:
- positions: float32 [16, 3, 6144], P('bead', None, 'dom')
- velocities: float32 [16, 3, 6144], P('bead', None, 'dom')
All inputs are finite; a program needn't handle non-finite values.
Results may differ from a plain program's by a relative error of at most 0.0003.
Values sent between devices are 32-bit elements; how exact they have to be, the bound alone decides.
A program may use at most 64 MiB of HBM per device.

v0:
```python
import jax
import jax.numpy as jnp
from jax import lax
from jax.sharding import PartitionSpec as P

BEADS = 16


KAPPA = 2.0
SOFTEN = 0.09
KICK = 0.3
OMEGA = 7.0
STEP_TIME = 0.1
HIGHEST = lax.Precision.HIGHEST


def from_behind(block, axis, distance):
    devices = range(lax.axis_size(axis))
    route = [((i - distance) % len(devices), i) for i in devices]
    return lax.ppermute(block, axis, route)


def mode_table(bead_index, mode_index):
    scale_root = jnp.sqrt(jnp.float32(BEADS))
    angle = 2.0 * jnp.pi * bead_index.astype(jnp.float32) * mode_index.astype(jnp.float32) / BEADS
    first = jnp.ones_like(angle) / scale_root
    middle = jnp.cos(jnp.pi * bead_index.astype(jnp.float32)) / scale_root + 0.0 * angle
    factor = jnp.sqrt(2.0 / jnp.float32(BEADS))
    return jnp.where(
        mode_index == 0,
        first,
        jnp.where(
            2 * mode_index < BEADS,
            factor * jnp.cos(angle),
            jnp.where(2 * mode_index == BEADS, middle, factor * jnp.sin(angle)),
        ),
    )


def evolve(mode_pos, mode_vel, mode_index):
    freq = 2.0 * OMEGA * jnp.sin(jnp.pi * mode_index.astype(jnp.float32) / BEADS)
    theta = freq * STEP_TIME
    cosine = jnp.cos(theta)[:, None, None]
    sine = jnp.sin(theta)
    safe_freq = jnp.where(mode_index > 0, freq, 1.0)
    carry_rate = jnp.where(mode_index > 0, sine / safe_freq, STEP_TIME)[:, None, None]
    new_pos = cosine * mode_pos + carry_rate * mode_vel
    new_vel = (-freq * sine)[:, None, None] * mode_pos + cosine * mode_vel
    return (new_pos, new_vel)


def pair_block(near_pos, near_charge, far_pack):
    far_pos = far_pack[:, :3]
    far_charge = far_pack[:, 3]
    delta = near_pos[:, :, :, None] - far_pos[:, :, None, :]
    square = jnp.sum(delta * delta, axis=1) + SOFTEN
    distance = jnp.sqrt(square)
    weight = (
        near_charge[None, :, None]
        * far_charge[:, None, :]
        * jnp.exp(-KAPPA * distance)
        * (1.0 + KAPPA * distance)
        / (square * distance)
    )
    terms = weight[:, None] * delta
    return (jnp.sum(terms, axis=3), -jnp.sum(terms, axis=2))


def block_force(near_pos, near_charge, far_pack, with_reaction):
    far_count = far_pack.shape[2]
    span_size = far_count
    while span_size > 512 and span_size % 2 == 0:
        span_size = span_size // 2

    def one_span(total, span_index):
        piece = lax.dynamic_slice_in_dim(far_pack, span_index * span_size, span_size, 2)
        force_part, react_part = pair_block(near_pos, near_charge, piece)
        return (total + force_part, react_part if with_reaction else None)

    total, reacts = lax.scan(
        one_span, jnp.zeros_like(near_pos), jnp.arange(far_count // span_size, dtype=jnp.int32)
    )
    if with_reaction:
        reacts = jnp.moveaxis(reacts, 0, 2).reshape(near_pos.shape[0], 3, far_count)
    return (total, reacts)


def local(mode_pos, mode_vel, charges):
    local_beads = mode_pos.shape[0]
    own_modes = lax.axis_index("bead") * local_beads + jnp.arange(local_beads, dtype=jnp.int32)
    new_pos, new_vel = evolve(mode_pos, mode_vel, own_modes)
    pieces = (
        lax.all_gather(new_pos, "bead", axis=0, tiled=True),
        lax.all_gather(new_vel, "bead", axis=0, tiled=True),
    )
    span_count = pieces[0].shape[0]
    columns = jnp.arange(span_count, dtype=jnp.int32)
    table = mode_table(own_modes[:, None], columns[None, :])
    first = jnp.einsum("bk,kcn->bcn", table, pieces[0], precision=HIGHEST)
    second = jnp.einsum("bk,kcn->bcn", table, pieces[1], precision=HIGHEST)
    charge_rows = jnp.broadcast_to(charges[None, None, :], (local_beads, 1, charges.shape[0]))
    packed = jnp.concatenate((first, charge_rows), axis=1)
    half_count = lax.axis_size("dom") // 2
    own_force, unused = block_force(first, charges, packed, False)

    def cycle_step(step_index, state):
        total, travel_pack, travel_react = state
        travel_pack, travel_react = from_behind((travel_pack, travel_react), "dom", 1)
        force_part, react_part = block_force(first, charges, travel_pack, True)
        keep = jnp.where(step_index < half_count, 1.0, 0.0).astype(first.dtype)
        return (total + force_part, travel_pack, travel_react + keep * react_part)

    total, unused_pack, travel_react = lax.fori_loop(
        1, half_count + 1, cycle_step, (own_force, packed, jnp.zeros_like(first))
    )
    forces = total + from_behind(travel_react, "dom", half_count)
    return (first, second + KICK * forces)


def solution(mesh):
    placed = (P("bead", None, "dom"), P("bead", None, "dom"), P("dom"))
    return jax.shard_map(
        local,
        mesh=mesh,
        in_specs=placed,
        out_specs=(P("bead", None, "dom"), P("bead", None, "dom")),
        check_vma=False,
    )
```

profile of v0, /device:TPU:0, one launch (start us, length us, event | category | flops | bytes accessed | tf_op | source)
XLA Modules:
  0.0 188.2 jit_solution(8247484512665379710)
XLA Ops:
  0.6 0.1 compare_select_fusion
  0.7 0.1 multiply_cosine_fusion
  1.0 1.5 multiply_add_fusion
  2.5 10.2 %all_gather.6 = f32[16,3,768]{2,1,0:T(4,128)S(1)} all-gather(f32[4,3,768]{2,1,0:T(4,128)S(1)} %copy.45), channel_id=1, replica_groups=mesh['bead'=4,'dom'=8] {'bead'}, dimensions={0}, use_global_device_ids=true | all-gather | bytes 184320 | tf_op jit(solution)/shard_map/all_gather | solution.py:93
  12.7 0.3 fusion.17
  13.0 0.7 broadcast_in_dim.48
  13.8 27.8 %while.59 = (s32[]{:T(128)}, f32[4,3,768]{2,1,0:T(4,128)S(1)}, f32[768]{0:T(1024)}, s32[2]{0:T(128)S(1)}, f32[4,4,768]{2,0,1:T(4,128)S(1)}, /*index=5*/f32[4,3,7...) while((s32[]{:T(128)}, f32[4,3,768]{2,1,0:T(4,128)S(1)}, ...), condition=%wide.region_3.4_spmd.clone, body=%wide.region_0.3_spmd.clone.sunk | while | flops 30680072 | bytes 19240164 | solution.py:80
  13.8 0.6 dynamic_slice.19
  15.1 4.3 %fusion.45 = f32[4,768,384]{2,1,0:T(8,128)} fusion(f32[4,3,384]{2,1,0:T(4,128)S(1)} %copy.66, f32[4,3,768]{2,1,0:T(4,128)S(1)} %get-tuple-element.572), kind=kLoop, calls=%fused_computation.19.clone.1 | loop fusion | flops 9437184 | bytes 4773888 | tf_op jit(solution)/shard_map/while/body/eval_jaxpr/reduce_sum | solution.py:56
  19.4 5.2 %fusion.46 = f32[4,768,384]{2,1,0:T(8,128)S(1)} fusion(f32[4,768,384]{2,1,0:T(8,128)} %fusion.45, f32[4,384]{1,0:T(4,128)S(1)} %dynamic-slice_bitcast_fusion.4, f32[768]{0:T(1024)S(1)} %copy-done), kind=kLoop, calls=%fused_computation.27.clone.1 | loop fusion | flops 10616832 | bytes 9446400 | tf_op jit(solution)/shard_map/while/body/eval_jaxpr/div | solution.py:59
  24.6 3.1 %fusion.47 = f32[4,3,768]{2,1,0:T(4,128)S(1)} fusion(f32[4,768,384]{2,1,0:T(8,128)S(1)} %fusion.46, f32[4,3,384]{2,1,0:T(4,128)S(1)} %copy.66, f32[4,3,768]{2,1,0:T(4,128)S(1)} %get-tuple-element.572), kind=kLoop, calls=%fused_computation.20.clone.1 | loop fusion | flops 10607616 | bytes 4810752 | tf_op jit(solution)/shard_map/while/body/eval_jaxpr/reduce_sum | solution.py:66
  27.7 0.6 dynamic_slice.19
  29.0 4.3 %fusion.45 = f32[4,768,384]{2,1,0:T(8,128)} fusion(f32[4,3,384]{2,1,0:T(4,128)S(1)} %copy.66, f32[4,3,768]{2,1,0:T(4,128)S(1)} %get-tuple-element.572), kind=kLoop, calls=%fused_computation.19.clone.1 | loop fusion | flops 9437184 | bytes 4773888 | tf_op jit(solution)/shard_map/while/body/eval_jaxpr/reduce_sum | solution.py:56
  33.3 5.2 %fusion.46 = f32[4,768,384]{2,1,0:T(8,128)S(1)} fusion(f32[4,768,384]{2,1,0:T(8,128)} %fusion.45, f32[4,384]{1,0:T(4,128)S(1)} %dynamic-slice_bitcast_fusion.4, f32[768]{0:T(1024)S(1)} %copy-done), kind=kLoop, calls=%fused_computation.27.clone.1 | loop fusion | flops 10616832 | bytes 9446400 | tf_op jit(solution)/shard_map/while/body/eval_jaxpr/div | solution.py:59
  38.5 3.1 %fusion.47 = f32[4,3,768]{2,1,0:T(4,128)S(1)} fusion(f32[4,768,384]{2,1,0:T(8,128)S(1)} %fusion.46, f32[4,3,384]{2,1,0:T(4,128)S(1)} %copy.66, f32[4,3,768]{2,1,0:T(4,128)S(1)} %get-tuple-element.572), kind=kLoop, calls=%fused_computation.20.clone.1 | loop fusion | flops 10607616 | bytes 4810752 | tf_op jit(solution)/shard_map/while/body/eval_jaxpr/reduce_sum | solution.py:66
  41.7 136.7 %while.61 = (s32[]{:T(128)}, f32[4,3,768]{2,1,0:T(4,128)S(1)}, f32[4,4,768]{2,0,1:T(4,128)S(1)}, f32[4,3,768]{2,0,1:T(4,128)S(1)}, f32[768]{0:T(1024)}, /*index=...) while((s32[]{:T(128)}, f32[4,3,768]{2,1,0:T(4,128)S(1)}, ...), condition=%wide.region_10.11_spmd.clone, body=%wide.region_4.10_spmd.clone.sunk | while | flops 34255880 | bytes 20266596 | solution.py:113
  41.7 0.1 collective-permute-start
  41.8 1.7 collective-permute-start.1
  43.5 3.6 %collective-permute-done = f32[4,4,768]{2,0,1:T(4,128)S(1)} collective-permute-done((f32[4,4,768]{2,0,1:T(4,128)S(1)}, f32[4,4,768]{2,0,1:T(4,128)S(1)}, u32[]{:S(2)}, u32[]{:S(2)}) %collective-permute-start) | collective-permute-done | bytes 49184 | tf_op jit(solution)/shard_map/while/body/eval_jaxpr/ppermute | solution.py:20
  47.0 28.6 %while.62 = (s32[]{:T(128)}, f32[4,3,768]{2,1,0:T(4,128)S(1)}, f32[2,4,3,384]{3,2,1,0:T(4,128)S(1)}, f32[768]{0:T(1024)}, s32[2]{0:T(128)S(1)}, /*index=5*/f32[4...) while((s32[]{:T(128)}, f32[4,3,768]{2,1,0:T(4,128)S(1)}, ...), condition=%wide.region_9.9_spmd.clone, body=%wide.region_5.8_spmd.clone.sunk | while | flops 34219016 | bytes 19307760 | solution.py:80
  47.1 0.6 dynamic_slice.20
  48.3 4.3 %fusion.48 = f32[4,768,384]{2,1,0:T(8,128)} fusion(f32[4,3,384]{2,1,0:T(4,128)S(1)} %copy.68, f32[4,3,768]{2,1,0:T(4,128)S(1)} %get-tuple-element.539), kind=kLoop, calls=%fused_computation.4.clone.1 | loop fusion | flops 9437184 | bytes 4773888 | tf_op jit(solution)/shard_map/while/body/eval_jaxpr/while/body/eval_jaxpr/reduce_sum | solution.py:56
  52.6 5.2 %fusion.49 = f32[4,768,384]{2,1,0:T(8,128)S(1)} fusion(f32[4,768,384]{2,1,0:T(8,128)} %fusion.48, f32[4,384]{1,0:T(4,128)S(1)} %dynamic-slice_bitcast_fusion.5, f32[768]{0:T(1024)S(1)} %copy-done.1), kind=kLoop, calls=%fused_computation.11.clone.1 | loop fusion | flops 10616832 | bytes 9446400 | tf_op jit(solution)/shard_map/while/body/eval_jaxpr/while/body/eval_jaxpr/div | solution.py:59
  57.8 3.5 %fusion.50 = (f32[4,3,384]{2,1,0:T(4,128)S(1)}, f32[4,3,768]{2,1,0:T(4,128)S(1)}) fusion(f32[4,768,384]{2,1,0:T(8,128)S(1)} %fusion.49, f32[4,3,384]{2,1,0:T(4,128)S(1)} %copy.68, f32[4,3,768]{2,1,0:T(4,128)S(1)} %get-tuple-element.539), kind=kLoop, calls=%fused_computation.2.clone.1 | loop fusion | flops 14141952 | bytes 4829184 | tf_op jit(solution)/shard_map/while/body/eval_jaxpr/while/body/eval_jaxpr/reduce_sum | solution.py:66
  61.4 0.6 dynamic_slice.20
  62.7 4.3 %fusion.48 = f32[4,768,384]{2,1,0:T(8,128)} fusion(f32[4,3,384]{2,1,0:T(4,128)S(1)} %copy.68, f32[4,3,768]{2,1,0:T(4,128)S(1)} %get-tuple-element.539), kind=kLoop, calls=%fused_computation.4.clone.1 | loop fusion | flops 9437184 | bytes 4773888 | tf_op jit(solution)/shard_map/while/body/eval_jaxpr/while/body/eval_jaxpr/reduce_sum | solution.py:56
  66.9 5.2 %fusion.49 = f32[4,768,384]{2,1,0:T(8,128)S(1)} fusion(f32[4,768,384]{2,1,0:T(8,128)} %fusion.48, f32[4,384]{1,0:T(4,128)S(1)} %dynamic-slice_bitcast_fusion.5, f32[768]{0:T(1024)S(1)} %copy-done.1), kind=kLoop, calls=%fused_computation.11.clone.1 | loop fusion | flops 10616832 | bytes 9446400 | tf_op jit(solution)/shard_map/while/body/eval_jaxpr/while/body/eval_jaxpr/div | solution.py:59
  72.1 3.5 %fusion.50 = (f32[4,3,384]{2,1,0:T(4,128)S(1)}, f32[4,3,768]{2,1,0:T(4,128)S(1)}) fusion(f32[4,768,384]{2,1,0:T(8,128)S(1)} %fusion.49, f32[4,3,384]{2,1,0:T(4,128)S(1)} %copy.68, f32[4,3,768]{2,1,0:T(4,128)S(1)} %get-tuple-element.539), kind=kLoop, calls=%fused_computation.2.clone.1 | loop fusion | flops 14141952 | bytes 4829184 | tf_op jit(solution)/shard_map/while/body/eval_jaxpr/while/body/eval_jaxpr/reduce_sum | solution.py:66
  75.9 0.1 collective-permute-start
  76.0 5.2 %collective-permute-done = f32[4,4,768]{2,0,1:T(4,128)S(1)} collective-permute-done((f32[4,4,768]{2,0,1:T(4,128)S(1)}, f32[4,4,768]{2,0,1:T(4,128)S(1)}, u32[]{:S(2)}, u32[]{:S(2)}) %collective-permute-start) | collective-permute-done | bytes 49184 | tf_op jit(solution)/shard_map/while/body/eval_jaxpr/ppermute | solution.py:20
  81.2 28.6 %while.62 = (s32[]{:T(128)}, f32[4,3,768]{2,1,0:T(4,128)S(1)}, f32[2,4,3,384]{3,2,1,0:T(4,128)S(1)}, f32[768]{0:T(1024)}, s32[2]{0:T(128)S(1)}, /*index=5*/f32[4...) while((s32[]{:T(128)}, f32[4,3,768]{2,1,0:T(4,128)S(1)}, ...), condition=%wide.region_9.9_spmd.clone, body=%wide.region_5.8_spmd.clone.sunk | while | flops 34219016 | bytes 19307760 | solution.py:80
  81.2 0.6 dynamic_slice.20
  82.5 4.3 %fusion.48 = f32[4,768,384]{2,1,0:T(8,128)} fusion(f32[4,3,384]{2,1,0:T(4,128)S(1)} %copy.68, f32[4,3,768]{2,1,0:T(4,128)S(1)} %get-tuple-element.539), kind=kLoop, calls=%fused_computation.4.clone.1 | loop fusion | flops 9437184 | bytes 4773888 | tf_op jit(solution)/shard_map/while/body/eval_jaxpr/while/body/eval_jaxpr/reduce_sum | solution.py:56
  86.8 5.2 %fusion.49 = f32[4,768,384]{2,1,0:T(8,128)S(1)} fusion(f32[4,768,384]{2,1,0:T(8,128)} %fusion.48, f32[4,384]{1,0:T(4,128)S(1)} %dynamic-slice_bitcast_fusion.5, f32[768]{0:T(1024)S(1)} %copy-done.1), kind=kLoop, calls=%fused_computation.11.clone.1 | loop fusion | flops 10616832 | bytes 9446400 | tf_op jit(solution)/shard_map/while/body/eval_jaxpr/while/body/eval_jaxpr/div | solution.py:59
  92.0 3.5 %fusion.50 = (f32[4,3,384]{2,1,0:T(4,128)S(1)}, f32[4,3,768]{2,1,0:T(4,128)S(1)}) fusion(f32[4,768,384]{2,1,0:T(8,128)S(1)} %fusion.49, f32[4,3,384]{2,1,0:T(4,128)S(1)} %copy.68, f32[4,3,768]{2,1,0:T(4,128)S(1)} %get-tuple-element.539), kind=kLoop, calls=%fused_computation.2.clone.1 | loop fusion | flops 14141952 | bytes 4829184 | tf_op jit(solution)/shard_map/while/body/eval_jaxpr/while/body/eval_jaxpr/reduce_sum | solution.py:66
  95.5 0.6 dynamic_slice.20
  96.8 4.3 %fusion.48 = f32[4,768,384]{2,1,0:T(8,128)} fusion(f32[4,3,384]{2,1,0:T(4,128)S(1)} %copy.68, f32[4,3,768]{2,1,0:T(4,128)S(1)} %get-tuple-element.539), kind=kLoop, calls=%fused_computation.4.clone.1 | loop fusion | flops 9437184 | bytes 4773888 | tf_op jit(solution)/shard_map/while/body/eval_jaxpr/while/body/eval_jaxpr/reduce_sum | solution.py:56
  101.1 5.2 %fusion.49 = f32[4,768,384]{2,1,0:T(8,128)S(1)} fusion(f32[4,768,384]{2,1,0:T(8,128)} %fusion.48, f32[4,384]{1,0:T(4,128)S(1)} %dynamic-slice_bitcast_fusion.5, f32[768]{0:T(1024)S(1)} %copy-done.1), kind=kLoop, calls=%fused_computation.11.clone.1 | loop fusion | flops 10616832 | bytes 9446400 | tf_op jit(solution)/shard_map/while/body/eval_jaxpr/while/body/eval_jaxpr/div | solution.py:59
  106.3 3.5 %fusion.50 = (f32[4,3,384]{2,1,0:T(4,128)S(1)}, f32[4,3,768]{2,1,0:T(4,128)S(1)}) fusion(f32[4,768,384]{2,1,0:T(8,128)S(1)} %fusion.49, f32[4,3,384]{2,1,0:T(4,128)S(1)} %copy.68, f32[4,3,768]{2,1,0:T(4,128)S(1)} %get-tuple-element.539), kind=kLoop, calls=%fused_computation.2.clone.1 | loop fusion | flops 14141952 | bytes 4829184 | tf_op jit(solution)/shard_map/while/body/eval_jaxpr/while/body/eval_jaxpr/reduce_sum | solution.py:66
  110.0 0.1 collective-permute-start
  110.1 0.1 collective-permute-start.1
  110.2 5.2 %collective-permute-done = f32[4,4,768]{2,0,1:T(4,128)S(1)} collective-permute-done((f32[4,4,768]{2,0,1:T(4,128)S(1)}, f32[4,4,768]{2,0,1:T(4,128)S(1)}, u32[]{:S(2)}, u32[]{:S(2)}) %collective-permute-start) | collective-permute-done | bytes 49184 | tf_op jit(solution)/shard_map/while/body/eval_jaxpr/ppermute | solution.py:20
  115.4 28.6 %while.62 = (s32[]{:T(128)}, f32[4,3,768]{2,1,0:T(4,128)S(1)}, f32[2,4,3,384]{3,2,1,0:T(4,128)S(1)}, f32[768]{0:T(1024)}, s32[2]{0:T(128)S(1)}, /*index=5*/f32[4...) while((s32[]{:T(128)}, f32[4,3,768]{2,1,0:T(4,128)S(1)}, ...), condition=%wide.region_9.9_spmd.clone, body=%wide.region_5.8_spmd.clone.sunk | while | flops 34219016 | bytes 19307760 | solution.py:80
  115.4 0.6 dynamic_slice.20
  116.7 4.3 %fusion.48 = f32[4,768,384]{2,1,0:T(8,128)} fusion(f32[4,3,384]{2,1,0:T(4,128)S(1)} %copy.68, f32[4,3,768]{2,1,0:T(4,128)S(1)} %get-tuple-element.539), kind=kLoop, calls=%fused_computation.4.clone.1 | loop fusion | flops 9437184 | bytes 4773888 | tf_op jit(solution)/shard_map/while/body/eval_jaxpr/while/body/eval_jaxpr/reduce_sum | solution.py:56
  121.0 5.2 %fusion.49 = f32[4,768,384]{2,1,0:T(8,128)S(1)} fusion(f32[4,768,384]{2,1,0:T(8,128)} %fusion.48, f32[4,384]{1,0:T(4,128)S(1)} %dynamic-slice_bitcast_fusion.5, f32[768]{0:T(1024)S(1)} %copy-done.1), kind=kLoop, calls=%fused_computation.11.clone.1 | loop fusion | flops 10616832 | bytes 9446400 | tf_op jit(solution)/shard_map/while/body/eval_jaxpr/while/body/eval_jaxpr/div | solution.py:59
  126.1 3.5 %fusion.50 = (f32[4,3,384]{2,1,0:T(4,128)S(1)}, f32[4,3,768]{2,1,0:T(4,128)S(1)}) fusion(f32[4,768,384]{2,1,0:T(8,128)S(1)} %fusion.49, f32[4,3,384]{2,1,0:T(4,128)S(1)} %copy.68, f32[4,3,768]{2,1,0:T(4,128)S(1)} %get-tuple-element.539), kind=kLoop, calls=%fused_computation.2.clone.1 | loop fusion | flops 14141952 | bytes 4829184 | tf_op jit(solution)/shard_map/while/body/eval_jaxpr/while/body/eval_jaxpr/reduce_sum | solution.py:66
  129.7 0.6 dynamic_slice.20
  131.0 4.3 %fusion.48 = f32[4,768,384]{2,1,0:T(8,128)} fusion(f32[4,3,384]{2,1,0:T(4,128)S(1)} %copy.68, f32[4,3,768]{2,1,0:T(4,128)S(1)} %get-tuple-element.539), kind=kLoop, calls=%fused_computation.4.clone.1 | loop fusion | flops 9437184 | bytes 4773888 | tf_op jit(solution)/shard_map/while/body/eval_jaxpr/while/body/eval_jaxpr/reduce_sum | solution.py:56
  135.3 5.2 %fusion.49 = f32[4,768,384]{2,1,0:T(8,128)S(1)} fusion(f32[4,768,384]{2,1,0:T(8,128)} %fusion.48, f32[4,384]{1,0:T(4,128)S(1)} %dynamic-slice_bitcast_fusion.5, f32[768]{0:T(1024)S(1)} %copy-done.1), kind=kLoop, calls=%fused_computation.11.clone.1 | loop fusion | flops 10616832 | bytes 9446400 | tf_op jit(solution)/shard_map/while/body/eval_jaxpr/while/body/eval_jaxpr/div | solution.py:59
  140.5 3.5 %fusion.50 = (f32[4,3,384]{2,1,0:T(4,128)S(1)}, f32[4,3,768]{2,1,0:T(4,128)S(1)}) fusion(f32[4,768,384]{2,1,0:T(8,128)S(1)} %fusion.49, f32[4,3,384]{2,1,0:T(4,128)S(1)} %copy.68, f32[4,3,768]{2,1,0:T(4,128)S(1)} %get-tuple-element.539), kind=kLoop, calls=%fused_computation.2.clone.1 | loop fusion | flops 14141952 | bytes 4829184 | tf_op jit(solution)/shard_map/while/body/eval_jaxpr/while/body/eval_jaxpr/reduce_sum | solution.py:66
  144.4 5.2 %collective-permute-done = f32[4,4,768]{2,0,1:T(4,128)S(1)} collective-permute-done((f32[4,4,768]{2,0,1:T(4,128)S(1)}, f32[4,4,768]{2,0,1:T(4,128)S(1)}, u32[]{:S(2)}, u32[]{:S(2)}) %collective-permute-start) | collective-permute-done | bytes 49184 | tf_op jit(solution)/shard_map/while/body/eval_jaxpr/ppermute | solution.py:20
  149.6 28.6 %while.62 = (s32[]{:T(128)}, f32[4,3,768]{2,1,0:T(4,128)S(1)}, f32[2,4,3,384]{3,2,1,0:T(4,128)S(1)}, f32[768]{0:T(1024)}, s32[2]{0:T(128)S(1)}, /*index=5*/f32[4...) while((s32[]{:T(128)}, f32[4,3,768]{2,1,0:T(4,128)S(1)}, ...), condition=%wide.region_9.9_spmd.clone, body=%wide.region_5.8_spmd.clone.sunk | while | flops 34219016 | bytes 19307760 | solution.py:80
  149.6 0.6 dynamic_slice.20
  150.9 4.3 %fusion.48 = f32[4,768,384]{2,1,0:T(8,128)} fusion(f32[4,3,384]{2,1,0:T(4,128)S(1)} %copy.68, f32[4,3,768]{2,1,0:T(4,128)S(1)} %get-tuple-element.539), kind=kLoop, calls=%fused_computation.4.clone.1 | loop fusion | flops 9437184 | bytes 4773888 | tf_op jit(solution)/shard_map/while/body/eval_jaxpr/while/body/eval_jaxpr/reduce_sum | solution.py:56
  155.1 5.2 %fusion.49 = f32[4,768,384]{2,1,0:T(8,128)S(1)} fusion(f32[4,768,384]{2,1,0:T(8,128)} %fusion.48, f32[4,384]{1,0:T(4,128)S(1)} %dynamic-slice_bitcast_fusion.5, f32[768]{0:T(1024)S(1)} %copy-done.1), kind=kLoop, calls=%fused_computation.11.clone.1 | loop fusion | flops 10616832 | bytes 9446400 | tf_op jit(solution)/shard_map/while/body/eval_jaxpr/while/body/eval_jaxpr/div | solution.py:59
  160.3 3.5 %fusion.50 = (f32[4,3,384]{2,1,0:T(4,128)S(1)}, f32[4,3,768]{2,1,0:T(4,128)S(1)}) fusion(f32[4,768,384]{2,1,0:T(8,128)S(1)} %fusion.49, f32[4,3,384]{2,1,0:T(4,128)S(1)} %copy.68, f32[4,3,768]{2,1,0:T(4,128)S(1)} %get-tuple-element.539), kind=kLoop, calls=%fused_computation.2.clone.1 | loop fusion | flops 14141952 | bytes 4829184 | tf_op jit(solution)/shard_map/while/body/eval_jaxpr/while/body/eval_jaxpr/reduce_sum | solution.py:66
  163.9 0.6 dynamic_slice.20
  165.2 4.3 %fusion.48 = f32[4,768,384]{2,1,0:T(8,128)} fusion(f32[4,3,384]{2,1,0:T(4,128)S(1)} %copy.68, f32[4,3,768]{2,1,0:T(4,128)S(1)} %get-tuple-element.539), kind=kLoop, calls=%fused_computation.4.clone.1 | loop fusion | flops 9437184 | bytes 4773888 | tf_op jit(solution)/shard_map/while/body/eval_jaxpr/while/body/eval_jaxpr/reduce_sum | solution.py:56
  169.5 5.2 %fusion.49 = f32[4,768,384]{2,1,0:T(8,128)S(1)} fusion(f32[4,768,384]{2,1,0:T(8,128)} %fusion.48, f32[4,384]{1,0:T(4,128)S(1)} %dynamic-slice_bitcast_fusion.5, f32[768]{0:T(1024)S(1)} %copy-done.1), kind=kLoop, calls=%fused_computation.11.clone.1 | loop fusion | flops 10616832 | bytes 9446400 | tf_op jit(solution)/shard_map/while/body/eval_jaxpr/while/body/eval_jaxpr/div | solution.py:59
  174.6 3.5 %fusion.50 = (f32[4,3,384]{2,1,0:T(4,128)S(1)}, f32[4,3,768]{2,1,0:T(4,128)S(1)}) fusion(f32[4,768,384]{2,1,0:T(8,128)S(1)} %fusion.49, f32[4,3,384]{2,1,0:T(4,128)S(1)} %copy.68, f32[4,3,768]{2,1,0:T(4,128)S(1)} %get-tuple-element.539), kind=kLoop, calls=%fused_computation.2.clone.1 | loop fusion | flops 14141952 | bytes 4829184 | tf_op jit(solution)/shard_map/while/body/eval_jaxpr/while/body/eval_jaxpr/reduce_sum | solution.py:66
  178.4 0.1 collective-permute-start.2
  178.5 8.7 %all_gather.7 = f32[16,3,768]{2,1,0:T(4,128)S(1)} all-gather(f32[4,3,768]{2,1,0:T(4,128)S(1)} %copy.47), channel_id=1, replica_groups=mesh['bead'=4,'dom'=8] {'bead'}, dimensions={0}, use_global_device_ids=true | all-gather | bytes 184320 | tf_op jit(solution)/shard_map/all_gather | solution.py:94
  187.3 0.9 fusion.20
  (155 shorter events, 1.6 us)
Async XLA Ops:
  0.9 12.9 %copy-start.4 = (f32[4]{0:T(128)}, f32[4]{0:T(128)S(1)}, u32[]{:S(2)}) copy-start(f32[4]{0:T(128)S(1)} %get-tuple-element.365) | copy-start | bytes 52
  0.9 12.9 %copy-start.6 = (f32[4]{0:T(128)}, f32[4]{0:T(128)S(1)}, u32[]{:S(2)}) copy-start(f32[4]{0:T(128)S(1)} %get-tuple-element.366) | copy-start | bytes 52
  0.9 12.9 %copy-start.8 = (pred[16]{0:T(512)(128)(4,1)}, pred[16]{0:T(512)(128)(4,1)S(1)}, u32[]{:S(2)}) copy-start(pred[16]{0:T(512)(128)(4,1)S(1)} %get-tuple-element.367) | copy-start | bytes 52
  0.9 12.9 %copy-start.10 = (pred[16]{0:T(512)(128)(4,1)}, pred[16]{0:T(512)(128)(4,1)S(1)}, u32[]{:S(2)}) copy-start(pred[16]{0:T(512)(128)(4,1)S(1)} %get-tuple-element.368) | copy-start | bytes 52
  0.9 12.9 %copy-start.12 = (pred[16]{0:T(512)(128)(4,1)}, pred[16]{0:T(512)(128)(4,1)S(1)}, u32[]{:S(2)}) copy-start(pred[16]{0:T(512)(128)(4,1)S(1)} %iota_compare_fusion) | copy-start | bytes 52
  0.9 12.9 %copy-start.14 = (f32[16]{0:T(128)}, f32[16]{0:T(128)S(1)}, u32[]{:S(2)}) copy-start(f32[16]{0:T(128)S(1)} %iota_convert_fusion) | copy-start | bytes 196
  13.0 0.8 copy-start.2
  13.8 5.6 %copy-start = (f32[768]{0:T(1024)S(1)}, f32[768]{0:T(1024)}, u32[]{:S(2)}) copy-start(f32[768]{0:T(1024)} %get-tuple-element.569) | copy-start | bytes 9220 | tf_op jit(solution)/shard_map/while
  27.7 5.6 %copy-start = (f32[768]{0:T(1024)S(1)}, f32[768]{0:T(1024)}, u32[]{:S(2)}) copy-start(f32[768]{0:T(1024)} %get-tuple-element.569) | copy-start | bytes 9220 | tf_op jit(solution)/shard_map/while
  41.6 136.9 %copy-start.3 = (f32[4,3,768]{2,0,1:T(4,128)S(1)}, f32[4,3,768]{2,0,1:T(4,128)}, u32[]{:S(2)}) copy-start(f32[4,3,768]{2,0,1:T(4,128)} %get-tuple-element.361) | copy-start | bytes 110596
  41.6 145.6 %copy-start.5 = (f32[4]{0:T(128)S(1)}, f32[4]{0:T(128)}, u32[]{:S(2)}) copy-start(f32[4]{0:T(128)} %copy-done.4) | copy-start | bytes 52
  41.6 145.6 %copy-start.7 = (f32[4]{0:T(128)S(1)}, f32[4]{0:T(128)}, u32[]{:S(2)}) copy-start(f32[4]{0:T(128)} %copy-done.6) | copy-start | bytes 52
  41.6 145.6 %copy-start.9 = (pred[16]{0:T(512)(128)(4,1)S(1)}, pred[16]{0:T(512)(128)(4,1)}, u32[]{:S(2)}) copy-start(pred[16]{0:T(512)(128)(4,1)} %copy-done.8) | copy-start | bytes 52
  41.6 145.6 %copy-start.11 = (pred[16]{0:T(512)(128)(4,1)S(1)}, pred[16]{0:T(512)(128)(4,1)}, u32[]{:S(2)}) copy-start(pred[16]{0:T(512)(128)(4,1)} %copy-done.10) | copy-start | bytes 52
  41.6 145.6 %copy-start.13 = (pred[16]{0:T(512)(128)(4,1)S(1)}, pred[16]{0:T(512)(128)(4,1)}, u32[]{:S(2)}) copy-start(pred[16]{0:T(512)(128)(4,1)} %copy-done.12) | copy-start | bytes 52
  41.7 145.6 %copy-start.15 = (f32[16]{0:T(128)S(1)}, f32[16]{0:T(128)}, u32[]{:S(2)}) copy-start(f32[16]{0:T(128)} %copy-done.14) | copy-start | bytes 196
  41.7 5.4 %collective-permute-start = (f32[4,4,768]{2,0,1:T(4,128)S(1)}, f32[4,4,768]{2,0,1:T(4,128)S(1)}, u32[]{:S(2)}, u32[]{:S(2)}) collective-permute-start(f32[4,4,768]{2,0,1:T(4,128)S(1)} %get-tuple-element.596), channel_id=1, source_target_pairs={{7,0},{0,1},{1,2},{2,3},{3,4},{4,5},{5,6},{6,7},{15,8},{8,9},{9,10... | collective-permute-start | bytes 147464 | tf_op jit(solution)/shard_map/while/body/eval_jaxpr/ppermute | solution.py:20
  41.8 34.0 %collective-permute-start.1 = (f32[4,3,768]{2,0,1:T(4,128)S(1)}, f32[4,3,768]{2,0,1:T(4,128)S(1)}, u32[]{:S(2)}, u32[]{:S(2)}) collective-permute-start(f32[4,3,768]{2,0,1:T(4,128)S(1)} %broadcast_select_fusion.2), channel_id=1, source_target_pairs={{7,0},{0,1},{1,2},{2,3},{3,4},{4,5},{5,6},{6,7},{15,8},{8,9},{9,10... | collective-permute-start | bytes 110600 | tf_op jit(solution)/shard_map/while/body/eval_jaxpr/ppermute | solution.py:20
  47.0 5.6 %copy-start.1 = (f32[768]{0:T(1024)S(1)}, f32[768]{0:T(1024)}, u32[]{:S(2)}) copy-start(f32[768]{0:T(1024)} %get-tuple-element.536) | copy-start | bytes 9220 | tf_op jit(solution)/shard_map/while/body/eval_jaxpr/while
  61.4 5.6 %copy-start.1 = (f32[768]{0:T(1024)S(1)}, f32[768]{0:T(1024)}, u32[]{:S(2)}) copy-start(f32[768]{0:T(1024)} %get-tuple-element.536) | copy-start | bytes 9220 | tf_op jit(solution)/shard_map/while/body/eval_jaxpr/while
  75.9 5.4 %collective-permute-start = (f32[4,4,768]{2,0,1:T(4,128)S(1)}, f32[4,4,768]{2,0,1:T(4,128)S(1)}, u32[]{:S(2)}, u32[]{:S(2)}) collective-permute-start(f32[4,4,768]{2,0,1:T(4,128)S(1)} %get-tuple-element.596), channel_id=1, source_target_pairs={{7,0},{0,1},{1,2},{2,3},{3,4},{4,5},{5,6},{6,7},{15,8},{8,9},{9,10... | collective-permute-start | bytes 147464 | tf_op jit(solution)/shard_map/while/body/eval_jaxpr/ppermute | solution.py:20
  75.9 34.0 %collective-permute-start.1 = (f32[4,3,768]{2,0,1:T(4,128)S(1)}, f32[4,3,768]{2,0,1:T(4,128)S(1)}, u32[]{:S(2)}, u32[]{:S(2)}) collective-permute-start(f32[4,3,768]{2,0,1:T(4,128)S(1)} %broadcast_select_fusion.2), channel_id=1, source_target_pairs={{7,0},{0,1},{1,2},{2,3},{3,4},{4,5},{5,6},{6,7},{15,8},{8,9},{9,10... | collective-permute-start | bytes 110600 | tf_op jit(solution)/shard_map/while/body/eval_jaxpr/ppermute | solution.py:20
  81.2 5.6 %copy-start.1 = (f32[768]{0:T(1024)S(1)}, f32[768]{0:T(1024)}, u32[]{:S(2)}) copy-start(f32[768]{0:T(1024)} %get-tuple-element.536) | copy-start | bytes 9220 | tf_op jit(solution)/shard_map/while/body/eval_jaxpr/while
  95.5 5.6 %copy-start.1 = (f32[768]{0:T(1024)S(1)}, f32[768]{0:T(1024)}, u32[]{:S(2)}) copy-start(f32[768]{0:T(1024)} %get-tuple-element.536) | copy-start | bytes 9220 | tf_op jit(solution)/shard_map/while/body/eval_jaxpr/while
  110.0 5.4 %collective-permute-start = (f32[4,4,768]{2,0,1:T(4,128)S(1)}, f32[4,4,768]{2,0,1:T(4,128)S(1)}, u32[]{:S(2)}, u32[]{:S(2)}) collective-permute-start(f32[4,4,768]{2,0,1:T(4,128)S(1)} %get-tuple-element.596), channel_id=1, source_target_pairs={{7,0},{0,1},{1,2},{2,3},{3,4},{4,5},{5,6},{6,7},{15,8},{8,9},{9,10... | collective-permute-start | bytes 147464 | tf_op jit(solution)/shard_map/while/body/eval_jaxpr/ppermute | solution.py:20
  110.1 34.0 %collective-permute-start.1 = (f32[4,3,768]{2,0,1:T(4,128)S(1)}, f32[4,3,768]{2,0,1:T(4,128)S(1)}, u32[]{:S(2)}, u32[]{:S(2)}) collective-permute-start(f32[4,3,768]{2,0,1:T(4,128)S(1)} %broadcast_select_fusion.2), channel_id=1, source_target_pairs={{7,0},{0,1},{1,2},{2,3},{3,4},{4,5},{5,6},{6,7},{15,8},{8,9},{9,10... | collective-permute-start | bytes 110600 | tf_op jit(solution)/shard_map/while/body/eval_jaxpr/ppermute | solution.py:20
  115.4 5.6 %copy-start.1 = (f32[768]{0:T(1024)S(1)}, f32[768]{0:T(1024)}, u32[]{:S(2)}) copy-start(f32[768]{0:T(1024)} %get-tuple-element.536) | copy-start | bytes 9220 | tf_op jit(solution)/shard_map/while/body/eval_jaxpr/while
  129.7 5.6 %copy-start.1 = (f32[768]{0:T(1024)S(1)}, f32[768]{0:T(1024)}, u32[]{:S(2)}) copy-start(f32[768]{0:T(1024)} %get-tuple-element.536) | copy-start | bytes 9220 | tf_op jit(solution)/shard_map/while/body/eval_jaxpr/while
  144.2 5.4 %collective-permute-start = (f32[4,4,768]{2,0,1:T(4,128)S(1)}, f32[4,4,768]{2,0,1:T(4,128)S(1)}, u32[]{:S(2)}, u32[]{:S(2)}) collective-permute-start(f32[4,4,768]{2,0,1:T(4,128)S(1)} %get-tuple-element.596), channel_id=1, source_target_pairs={{7,0},{0,1},{1,2},{2,3},{3,4},{4,5},{5,6},{6,7},{15,8},{8,9},{9,10... | collective-permute-start | bytes 147464 | tf_op jit(solution)/shard_map/while/body/eval_jaxpr/ppermute | solution.py:20
  144.3 34.0 %collective-permute-start.1 = (f32[4,3,768]{2,0,1:T(4,128)S(1)}, f32[4,3,768]{2,0,1:T(4,128)S(1)}, u32[]{:S(2)}, u32[]{:S(2)}) collective-permute-start(f32[4,3,768]{2,0,1:T(4,128)S(1)} %broadcast_select_fusion.2), channel_id=1, source_target_pairs={{7,0},{0,1},{1,2},{2,3},{3,4},{4,5},{5,6},{6,7},{15,8},{8,9},{9,10... | collective-permute-start | bytes 110600 | tf_op jit(solution)/shard_map/while/body/eval_jaxpr/ppermute | solution.py:20
  149.6 5.6 %copy-start.1 = (f32[768]{0:T(1024)S(1)}, f32[768]{0:T(1024)}, u32[]{:S(2)}) copy-start(f32[768]{0:T(1024)} %get-tuple-element.536) | copy-start | bytes 9220 | tf_op jit(solution)/shard_map/while/body/eval_jaxpr/while
  163.9 5.6 %copy-start.1 = (f32[768]{0:T(1024)S(1)}, f32[768]{0:T(1024)}, u32[]{:S(2)}) copy-start(f32[768]{0:T(1024)} %get-tuple-element.536) | copy-start | bytes 9220 | tf_op jit(solution)/shard_map/while/body/eval_jaxpr/while
  178.4 8.8 %collective-permute-start.2 = (f32[4,3,768]{2,0,1:T(4,128)S(1)}, f32[4,3,768]{2,0,1:T(4,128)S(1)}, u32[]{:S(2)}, u32[]{:S(2)}) collective-permute-start(f32[4,3,768]{2,0,1:T(4,128)S(1)} %get-tuple-element.184), channel_id=1, source_target_pairs={{4,0},{5,1},{6,2},{7,3},{0,4},{1,5},{2,6},{3,7},{12,8},{13,9},{14,... | collective-permute-start | bytes 110600 | tf_op jit(solution)/shard_map/ppermute | solution.py:20
where the time goes:
time: 189 us; the launch traced here: 188 us
  other arithmetic  131 us (69%)
  waiting for transfers between devices  19.1 us (10%)
  blocking collectives  18.9 us (10%)
  loops' own time  7.51 us (4%)
  local copies, waits for them, and re-layouts  7.4 us (4%)
  starting transfers between devices  2.2 us (1%)
    div x10, other arithmetic, pair_block(): near_charge[None, :, None] * far_charge[:, None, :]  51.7 us
    reduce_sum x10, other arithmetic, pair_block(): square = jnp.sum(delta * delta, axis=1) + SOFTEN  42.7 us
    reduce_sum x10, other arithmetic, pair_block(): return (jnp.sum(terms, axis=3), -jnp.sum(terms, axis=2))  34 us
    ppermute x9, waiting for transfers between devices, from_behind(): return lax.ppermute(block, axis, route)  19.1 us
    all_gather x1, blocking collectives, local(): lax.all_gather(new_pos, 'bead', axis=0, tiled=True)  10.2 us
    all_gather x1, blocking collectives, local(): lax.all_gather(new_vel, 'bead', axis=0, tiled=True)  8.71 us
    another operation x5, loops' own time, block_force(): lax.scan(one_span, jnp.zeros_like(near_pos), jnp.arange(far_count // span...  7.03 us
    dynamic_slice x10, local copies, waits for them, and re-layouts, block_force(): lax.scan(one_span, jnp.zeros_like(near_pos), jnp.arange(far_count // span...  6.1 us
  transfers between devices with their start and end apart: 9, of which 4 were waited for; matrix products, arithmetic and copies ran while one was open for 58% of the time, Pallas kernels for 0%

commit v1 on v0

v1 whole, which is shorter than its diff:
```python
import functools

import jax
import jax.numpy as jnp
from jax import lax
from jax.experimental import pallas as pl
from jax.experimental.pallas import tpu as pltpu
from jax.sharding import PartitionSpec as P

BEADS = 16


KAPPA = 2.0
SOFTEN = 0.09
KICK = 0.3
OMEGA = 7.0
STEP_TIME = 0.1
HIGHEST = lax.Precision.HIGHEST
LOG2E = 1.4426950408889634
ROWS = 256


def mode_table(bead_index, mode_index):
    scale_root = jnp.sqrt(jnp.float32(BEADS))
    angle = 2.0 * jnp.pi * bead_index.astype(jnp.float32) * mode_index.astype(jnp.float32) / BEADS
    first = jnp.ones_like(angle) / scale_root
    middle = jnp.cos(jnp.pi * bead_index.astype(jnp.float32)) / scale_root + 0.0 * angle
    factor = jnp.sqrt(2.0 / jnp.float32(BEADS))
    return jnp.where(
        mode_index == 0,
        first,
        jnp.where(
            2 * mode_index < BEADS,
            factor * jnp.cos(angle),
            jnp.where(2 * mode_index == BEADS, middle, factor * jnp.sin(angle)),
        ),
    )


def evolve(mode_pos, mode_vel, mode_index):
    freq = 2.0 * OMEGA * jnp.sin(jnp.pi * mode_index.astype(jnp.float32) / BEADS)
    theta = freq * STEP_TIME
    cosine = jnp.cos(theta)[:, None, None]
    sine = jnp.sin(theta)
    safe_freq = jnp.where(mode_index > 0, freq, 1.0)
    carry_rate = jnp.where(mode_index > 0, sine / safe_freq, STEP_TIME)[:, None, None]
    new_pos = cosine * mode_pos + carry_rate * mode_vel
    new_vel = (-freq * sine)[:, None, None] * mode_pos + cosine * mode_vel
    return (new_pos, new_vel)


def split3(value):
    one = value.astype(jnp.bfloat16).astype(jnp.float32)
    rest = value - one
    two = rest.astype(jnp.bfloat16).astype(jnp.float32)
    return one, two, rest - two


def row_index(shape):
    return lax.broadcasted_iota(jnp.int32, shape, 0)


def scaled(pack, centre):
    return jnp.where(row_index(pack.shape) < 3, KAPPA * (pack - centre), 0.0)


def near_operand(pos):
    row = row_index(pos.shape)
    norm = jnp.sum(pos * pos, axis=0, keepdims=True) + KAPPA * KAPPA * SOFTEN
    one, two, three = split3(jnp.where(row == 3, norm, -2.0 * pos))
    last = row == 3
    groups = (
        one,
        jnp.where(last, two, one),
        jnp.where(last, three, two),
        jnp.where(last, 1.0, two),
        jnp.where(last, 1.0, one),
        jnp.where(last, 1.0, three),
    )
    return jnp.concatenate(groups, axis=0).astype(jnp.bfloat16)


def far_operands(pos, charge):
    row = row_index(pos.shape)
    last = row == 3
    norm = jnp.sum(pos * pos, axis=0, keepdims=True)
    one, two, three = split3(jnp.where(last, norm, pos))
    first = jnp.where(last, 1.0, one)
    groups = (
        first,
        jnp.where(last, 1.0, two),
        first,
        jnp.where(last, one, two),
        jnp.where(last, two, three),
        jnp.where(last, three, one),
    )
    left = jnp.concatenate(groups, axis=0).T.astype(jnp.bfloat16)
    moments = jnp.where(last, charge, pos * charge)
    parts = split3(moments) + (jnp.zeros_like(pos),)
    right = jnp.concatenate(parts, axis=0).astype(jnp.bfloat16)
    return left, right


def pair_weight(square):
    inverse = lax.rsqrt(square)
    decay = jnp.exp2(square * (inverse * (-LOG2E)))
    return decay * (1.0 + inverse) * (inverse * inverse)


def force_sums(left, right, near):
    total = None
    for start in range(0, left.shape[0], ROWS):
        square = jnp.dot(left[start : start + ROWS], near, preferred_element_type=jnp.float32)
        weight = pair_weight(square)
        high = weight.astype(jnp.bfloat16)
        low = (weight - high.astype(jnp.float32)).astype(jnp.bfloat16)
        moment = right[:, start : start + ROWS]
        part = jnp.dot(moment, high, preferred_element_type=jnp.float32)
        part += jnp.dot(moment, low, preferred_element_type=jnp.float32)
        total = part if total is None else total + part
    return total


def kernel(near_ref, far_ref, vel_ref, out_ref):
    beads, blocks = near_ref.shape[0], far_ref.shape[0]

    def one_bead(b, unused):
        pack = near_ref[b]
        centre = jnp.mean(pack, axis=1, keepdims=True)
        pos = scaled(pack, centre)
        near = near_operand(pos)

        def one_block(f, total):
            far = far_ref[f, b]
            left, right = far_operands(scaled(far, centre), far[3:4])
            return total + force_sums(left, right, near)

        total = lax.fori_loop(
            0, blocks, one_block, jnp.zeros((32, pack.shape[1]), jnp.float32)
        )
        sums = total[:8] + total[8:16] + total[16:24]
        force = (4.0 * KICK) * pack[3:4] * (pos * sums[3:4] - sums)
        out_ref[b] = vel_ref[b] + force[:3]
        return unused

    lax.fori_loop(0, beads, one_bead, 0)


def local(mode_pos, mode_vel, charges):
    local_beads = mode_pos.shape[0]
    own_modes = lax.axis_index("bead") * local_beads + jnp.arange(local_beads, dtype=jnp.int32)
    new_pos, new_vel = evolve(mode_pos, mode_vel, own_modes)
    both = lax.all_gather(jnp.concatenate((new_pos, new_vel), axis=1), "bead", axis=0, tiled=True)
    columns = jnp.arange(both.shape[0], dtype=jnp.int32)
    table = mode_table(own_modes[:, None], columns[None, :])
    mixed = jnp.einsum("bk,kcn->bcn", table, both, precision=HIGHEST)
    first, second = mixed[:, :3], mixed[:, 3:]
    count = charges.shape[0]
    charge_rows = jnp.broadcast_to(charges[None, None, :], (local_beads, 1, count))
    spare = jnp.zeros((local_beads, 4, count), jnp.float32)
    packed = jnp.concatenate((first, charge_rows, spare), axis=1)
    far = lax.all_gather(packed, "dom", axis=0)
    velocities = pl.pallas_call(
        kernel,
        out_shape=jax.ShapeDtypeStruct(first.shape, jnp.float32),
        in_specs=[pl.BlockSpec(memory_space=pltpu.VMEM)] * 3,
        out_specs=pl.BlockSpec(memory_space=pltpu.VMEM),
        compiler_params=pltpu.CompilerParams(vmem_limit_bytes=48 * 1024 * 1024),
    )(packed, far, second)
    return (first, velocities)


def solution(mesh):
    placed = (P("bead", None, "dom"), P("bead", None, "dom"), P("dom"))
    return jax.shard_map(
        local,
        mesh=mesh,
        in_specs=placed,
        out_specs=(P("bead", None, "dom"), P("bead", None, "dom")),
        check_vma=False,
    )
```

time: 189 us -> 85.4 us (0.45)
  other arithmetic: 131 us -> 1.19 us
  Pallas kernels: 0 us -> 53.3 us
  waiting for transfers between devices: 19.1 us -> 0 us
  blocking collectives: 18.9 us -> 27.4 us
  loops' own time: 7.51 us -> 0 us
  local copies, waits for them, and re-layouts: 7.4 us -> 2.05 us
  starting transfers between devices: 2.2 us -> 0 us
    reduce_sum x20 -> x0, other arithmetic: 76.7 us -> none  [the longest x10 42.7 us: pair_block(): square = jnp.sum(delta * delta, axis=1) + SOFTEN]
    pallas_call x0 -> x1, Pallas kernels: none -> 53.3 us  [local(): pl.pallas_call(kernel, out_shape=jax.ShapeDtypeStruct(first.shape, jnp.fl...]
    div x10 -> x0, other arithmetic: 51.7 us -> none  [pair_block(): near_charge[None, :, None] * far_charge[:, None, :]]
    ppermute x9 -> x0, waiting for transfers between devices: 19.1 us -> none  [from_behind(): return lax.ppermute(block, axis, route)]
    all_gather x2, blocking collectives: 18.9 us -> 27.4 us  [the longest x1 16.5 us: local(): far = lax.all_gather(packed, 'dom', axis=0)]
    another operation x6 -> x0, loops' own time: 7.51 us -> none  [the longest x5 7.03 us: block_force(): lax.scan(one_span, jnp.zeros_like(near_pos), jnp.arange(far_count // span...]
    dynamic_slice x10 -> x0, local copies, waits for them, and re-layouts: 6.1 us -> none  [block_force(): lax.scan(one_span, jnp.zeros_like(near_pos), jnp.arange(far_count // span...]
    ppermute x9 -> x0, starting transfers between devices: 2.2 us -> none  [from_behind(): return lax.ppermute(block, axis, route)]
  transfers between devices with their start and end apart: 9 -> 0, of which waited for: 4 -> 0; matrix products, arithmetic and copies ran while one was open for 58% -> 0% of each run, Pallas kernels for 0% -> 0%
where the time goes in v1:
time: 85.4 us; the launch traced here: 85.2 us
  Pallas kernels  53.3 us (62%)
  blocking collectives  27.4 us (32%)
  local copies, waits for them, and re-layouts  2.05 us (2%)
  other arithmetic  1.19 us (1%)
    pallas_call x1, Pallas kernels, local(): pl.pallas_call(kernel, out_shape=jax.ShapeDtypeStruct(first.shape, jnp.fl...  53.3 us
    all_gather x1, blocking collectives, local(): far = lax.all_gather(packed, 'dom', axis=0)  16.5 us
    all_gather x1, blocking collectives, local(): lax.all_gather(jnp.concatenate((new_pos, new_vel), axis=1), 'bead', axis=...  11 us

profile of v1, /device:TPU:0, one launch (start us, length us, event | category | flops | bytes accessed | tf_op | source)
XLA Modules:
  0.0 85.2 jit_solution(5730545683317553364)
XLA Ops:
  0.6 0.0 copy-start.1
  0.6 0.1 multiply_cosine_fusion
  0.7 0.1 pad.2.clone
  0.8 0.1 compare_select_fusion
  1.0 0.7 broadcast_in_dim.41
  1.7 0.0 copy-done.1
  1.7 0.9 %multiply_add_fusion.1 = (f32[4,3,768]{2,0,1:T(4,128)S(1)}, f32[4,3,768]{2,0,1:T(4,128)S(1)}) fusion(f32[4,3,768]{2,0,1:T(4,128)S(1)} %copy-done.1, f32[4,3,768]{2,0,1:T(4,128)} %param.3, f32[4]{0:T(128)S(1)} %get-tuple-element.12, f32[4]{0:T(128)S(1)} %multiply_cosine_fusion, f32[4]{0:T(128)S(1)} %get-tuple-element.13), kind=kLoop, calls=%fused_computation.5 | loop fusion | flops 55296 | bytes 147504 | tf_op jit(solution)/shard_map/add | solution.py:47
  2.6 11.0 %all_gather.9 = f32[16,6,768]{2,1,0:T(8,128)S(1)} all-gather(f32[4,6,768]{2,1,0:T(8,128)S(1)} %copy.18), channel_id=1, replica_groups=mesh['bead'=4,'dom'=8] {'bead'}, dimensions={0}, use_global_device_ids=true | all-gather | bytes 368640 | tf_op jit(solution)/shard_map/all_gather | solution.py:153
  13.6 0.4 fusion
  14.0 0.0 copy-start
  14.1 0.6 copy-done
  14.7 0.1 maximum_maximum_fusion.near_ref
  14.7 16.5 %all-gather = f32[32,8,768]{2,1,0:T(8,128)S(1)} all-gather(f32[4,8,768]{2,1,0:T(8,128)S(1)} %maximum_maximum_fusion.near_ref), channel_id=2, replica_groups=mesh['bead'=4,'dom'=8] {'dom'}, dimensions={0}, use_global_device_ids=true | all-gather | bytes 884736 | tf_op jit(solution)/shard_map/all_gather | solution.py:162
  31.2 53.3 %shard_map.50 = f32[4,3,768]{2,1,0:T(4,128)S(1)} custom-call(f32[4,8,768]{2,1,0:T(8,128)S(1)} %maximum_maximum_fusion.near_ref, f32[8,4,8,768]{3,2,1,0:T(8,128)S(1)} %bitcast.4, f32[4,3,768]{2,1,0:T(4,128)S(1)} %copy.25.vel_ref), custom_call_target="tpu_custom_call" | custom-call | tf_op jit(solution)/shard_map/pallas_call | solution.py:163
  84.5 0.6 copy.23
  (10 shorter events, 0.1 us)
Async XLA Ops:
  0.6 1.0 %copy-start.1 = (f32[4,3,768]{2,0,1:T(4,128)S(1)}, f32[4,3,768]{2,0,1:T(4,128)}, u32[]{:S(2)}) copy-start(f32[4,3,768]{2,0,1:T(4,128)} %param.4) | copy-start | bytes 110596
  14.0 0.6 copy-start

commit v2 on v1

v2 whole, which is shorter than its diff:
```python
import functools

import jax
import jax.numpy as jnp
import numpy as np
from jax import lax
from jax.experimental import pallas as pl
from jax.experimental.pallas import tpu as pltpu
from jax.sharding import PartitionSpec as P

KAPPA = 2.0
SOFTEN = 0.09
KICK = 0.3
OMEGA = 7.0
STEP_TIME = 0.1
LOG2E = 1.4426950408889634
ROWS = 256
MESH = pl.DeviceIdType.MESH


def mode_table(beads):
    bead, mode = np.arange(beads)[:, None], np.arange(beads)[None, :]
    angle = 2.0 * np.pi * bead * mode / beads
    wave = np.where(2 * mode < beads, np.cos(angle), np.sin(angle)) * np.sqrt(2.0 / beads)
    edge = np.where(mode == 0, 1.0, np.cos(np.pi * bead)) / np.sqrt(beads)
    return np.where((mode == 0) | (2 * mode == beads), edge, wave).astype(np.float32)


def step_table(beads):
    freq = 2.0 * OMEGA * np.sin(np.pi * np.arange(beads) / beads)
    theta = freq * STEP_TIME
    rate = np.where(freq > 0, np.sin(theta) / np.where(freq > 0, freq, 1.0), STEP_TIME)
    return np.stack((np.cos(theta), rate, -freq * np.sin(theta)), axis=1).astype(np.float32)


def split3(value):
    one = value.astype(jnp.bfloat16).astype(jnp.float32)
    rest = value - one
    two = rest.astype(jnp.bfloat16).astype(jnp.float32)
    return one, two, rest - two


def row_index(shape):
    return lax.broadcasted_iota(jnp.int32, shape, 0)


def scaled(pack, centre):
    return jnp.where(row_index(pack.shape) < 3, KAPPA * (pack - centre), 0.0)


def near_operand(pos):
    row = row_index(pos.shape)
    norm = jnp.sum(pos * pos, axis=0, keepdims=True) + KAPPA * KAPPA * SOFTEN
    one, two, three = split3(jnp.where(row == 3, norm, -2.0 * pos))
    last = row == 3
    groups = (
        one,
        jnp.where(last, two, one),
        jnp.where(last, three, two),
        jnp.where(last, 1.0, two),
        jnp.where(last, 1.0, one),
        jnp.where(last, 1.0, three),
    )
    return jnp.concatenate(groups, axis=0).astype(jnp.bfloat16)


def moment_parts(pos, charge):
    moments = jnp.where(row_index(pos.shape) == 3, charge, pos * charge)
    return jnp.concatenate(split3(moments) + (jnp.zeros_like(pos),), axis=0)


def far_operand(pos):
    last = row_index(pos.shape) == 3
    norm = jnp.sum(pos * pos, axis=0, keepdims=True)
    one, two, three = split3(jnp.where(last, norm, pos))
    first = jnp.where(last, 1.0, one)
    groups = (
        first,
        jnp.where(last, 1.0, two),
        first,
        jnp.where(last, one, two),
        jnp.where(last, two, three),
        jnp.where(last, three, one),
    )
    return jnp.concatenate(groups, axis=0).T.astype(jnp.bfloat16)


def pair_weight(square):
    inverse = lax.rsqrt(square)
    decay = jnp.exp2(square * (inverse * (-LOG2E)))
    return decay * (1.0 + inverse) * (inverse * inverse)


def block_sums(left, right, near, near_moment):
    total, backs = None, []
    for start in range(0, left.shape[0], ROWS):
        square = jnp.dot(left[start : start + ROWS], near, preferred_element_type=jnp.float32)
        weight = pair_weight(square)
        high = weight.astype(jnp.bfloat16)
        low = (weight - high.astype(jnp.float32)).astype(jnp.bfloat16)
        moment = right[:, start : start + ROWS]
        part = jnp.dot(moment, high, preferred_element_type=jnp.float32)
        part += jnp.dot(moment, low, preferred_element_type=jnp.float32)
        total = part if total is None else total + part
        if near_moment is not None:
            back = jnp.dot(high, near_moment, preferred_element_type=jnp.float32)
            back += jnp.dot(low, near_moment, preferred_element_type=jnp.float32)
            backs.append(back)
    back = jnp.concatenate(backs, axis=0).T if backs else None
    return total, back


def force_of(pos, charge, sums):
    sums = sums[:8] + sums[8:16] + sums[16:24]
    return (4.0 * KICK) * charge * (pos * sums[3:4] - sums)


def kernel(
    n_bead, n_dom, table_ref, step_ref, pos_ref, vel_ref, charge_ref, pos_out, vel_out,
    modes, packs, speed, centres, near_ops, near_moments, sums, backs, returned,
    mode_send, mode_recv, pack_send, pack_recv, back_send, back_recv,
):
    me_bead, me = lax.axis_index("bead"), lax.axis_index("dom")
    beads, half = pos_ref.shape[0], n_dom // 2
    part = beads // 2
    tile = (8, pos_ref.shape[2])
    row = row_index(tile)

    barrier = pltpu.get_barrier_semaphore()
    for step in range(1, n_bead):
        pl.semaphore_signal(
            barrier, inc=1, device_id={"bead": lax.rem(me_bead + step, n_bead)}, device_id_type=MESH
        )
    for step in range(1, n_dom):
        pl.semaphore_signal(
            barrier, inc=1, device_id={"dom": lax.rem(me + step, n_dom)}, device_id_type=MESH
        )

    for k in range(beads):
        mode = me_bead * beads + k
        old_pos, old_vel = pos_ref[k], vel_ref[k]
        modes[0, k] = jnp.zeros(tile, jnp.float32)
        modes[0, k, 0:3] = step_ref[mode, 0] * old_pos + step_ref[mode, 1] * old_vel
        modes[0, k, 4:7] = step_ref[mode, 2] * old_pos + step_ref[mode, 0] * old_vel
    pl.semaphore_wait(barrier, n_bead + n_dom - 2)

    def mode_copy(step):
        return pltpu.make_async_remote_copy(
            src_ref=modes.at[0], dst_ref=modes.at[step],
            send_sem=mode_send.at[step], recv_sem=mode_recv.at[step],
            device_id={"bead": lax.rem(me_bead + step, n_bead)}, device_id_type=MESH,
        )

    for step in range(1, n_bead):
        mode_copy(step).start()
    mixed = [jnp.zeros(tile, jnp.float32) for b in range(beads)]
    for step in range(n_bead):
        if step:
            mode_copy(step).wait_recv()
        first = lax.rem(me_bead - step + n_bead, n_bead) * beads
        for k in range(beads):
            mode = modes[step, k]
            for b in range(beads):
                mixed[b] = mixed[b] + table_ref[me_bead * beads + b, first + k] * mode

    charge = charge_ref[...]
    for b in range(beads):
        packs[0, b] = jnp.where(row < 3, mixed[b], jnp.where(row == 3, charge, 0.0))

    def pack_copy(step):
        return pltpu.make_async_remote_copy(
            src_ref=packs.at[0], dst_ref=packs.at[step],
            send_sem=pack_send.at[step], recv_sem=pack_recv.at[step],
            device_id={"dom": lax.rem(me + step, n_dom)}, device_id_type=MESH,
        )

    for step in range(1, half + 1):
        pack_copy(step).start()
    for b in range(beads):
        pos_out[b] = mixed[b][:3]
        speed[b] = pltpu.roll(mixed[b], 4, axis=0)
        pack = packs[0, b]
        centre = jnp.broadcast_to(jnp.mean(pack, axis=1, keepdims=True), tile)
        centres[b] = centre
        pos = scaled(pack, centre)
        near_ops[b] = near_operand(pos)
        near_moments[b] = moment_parts(pos, charge).T.astype(jnp.bfloat16)
        sums[b] = jnp.zeros((32, tile[1]), jnp.float32)

    def one_unit(step, b, with_back):
        pack = packs[step, b]
        pos = scaled(pack, centres[b])
        right = moment_parts(pos, pack[3:4]).astype(jnp.bfloat16)
        moment = near_moments[b] if with_back else None
        total, back = block_sums(far_operand(pos), right, near_ops[b], moment)
        sums[b] += total
        if with_back:
            backs[step, b] = force_of(pos, pack[3:4], back)

    def own_unit(b, unused):
        one_unit(0, b, False)
        return unused

    mine = jnp.where(me < half, 0, part)
    theirs = part - mine

    def back_copy(step):
        span = pl.ds(0, beads)
        return pltpu.make_async_remote_copy(
            src_ref=backs.at[step, span], dst_ref=returned.at[step, span],
            send_sem=back_send.at[step], recv_sem=back_recv.at[step],
            device_id={"dom": lax.rem(me - step + n_dom, n_dom)}, device_id_type=MESH,
        )

    def last_copy(first):
        span = pl.ds(first, part)
        return pltpu.make_async_remote_copy(
            src_ref=backs.at[half, span], dst_ref=returned.at[half, span],
            send_sem=back_send.at[half], recv_sem=back_recv.at[half],
            device_id={"dom": lax.rem(me - half + n_dom, n_dom)}, device_id_type=MESH,
        )

    lax.fori_loop(0, part, own_unit, 0)

    def one_step(step, unused):
        pack_copy(step).wait_recv()
        first = jnp.where(step < half, 0, mine)
        count = jnp.where(step < half, beads, part)

        def unit(b, inner):
            one_unit(step, first + b, True)
            return inner

        lax.fori_loop(0, count, unit, 0)

        @pl.when(step < half)
        def _():
            back_copy(step).start()

        return unused

    lax.fori_loop(1, half + 1, one_step, 0)
    last_copy(mine).start()
    lax.fori_loop(part, beads, own_unit, 0)

    for b in range(beads):
        pack = packs[0, b]
        pos = scaled(pack, centres[b])
        speed[b] += force_of(pos, pack[3:4], sums[b])

    def collect(step, unused):
        back_copy(step).wait_recv()
        for b in range(beads):
            speed[b] += returned[step, b]
        return unused

    lax.fori_loop(1, half, collect, 0)
    last_copy(theirs).wait_recv()
    for b in range(part):
        speed[theirs + b] += returned[half, theirs + b]
    for b in range(beads):
        vel_out[b] = speed[b, 0:3]

    for step in range(1, n_bead):
        mode_copy(step).wait_send()
    for step in range(1, half + 1):
        pack_copy(step).wait_send()
    for step in range(1, half):
        back_copy(step).wait_send()
    last_copy(mine).wait_send()


def local(mode_pos, mode_vel, charges):
    n_bead, n_dom = lax.axis_size("bead"), lax.axis_size("dom")
    beads, unused, count = mode_pos.shape
    half = n_dom // 2
    total = n_bead * beads
    vmem, smem = pl.BlockSpec(memory_space=pltpu.VMEM), pl.BlockSpec(memory_space=pltpu.SMEM)
    shape = jax.ShapeDtypeStruct(mode_pos.shape, jnp.float32)
    return pl.pallas_call(
        functools.partial(kernel, n_bead, n_dom),
        out_shape=(shape, shape),
        in_specs=[smem, smem, vmem, vmem, vmem],
        out_specs=(vmem, vmem),
        scratch_shapes=[
            pltpu.VMEM((n_bead, beads, 8, count), jnp.float32),
            pltpu.VMEM((half + 1, beads, 8, count), jnp.float32),
            pltpu.VMEM((beads, 8, count), jnp.float32),
            pltpu.VMEM((beads, 8, count), jnp.float32),
            pltpu.VMEM((beads, 48, count), jnp.bfloat16),
            pltpu.VMEM((beads, count, 32), jnp.bfloat16),
            pltpu.VMEM((beads, 32, count), jnp.float32),
            pltpu.VMEM((half + 1, beads, 8, count), jnp.float32),
            pltpu.VMEM((half + 1, beads, 8, count), jnp.float32),
            pltpu.SemaphoreType.DMA((n_bead,)),
            pltpu.SemaphoreType.DMA((n_bead,)),
            pltpu.SemaphoreType.DMA((half + 1,)),
            pltpu.SemaphoreType.DMA((half + 1,)),
            pltpu.SemaphoreType.DMA((half + 1,)),
            pltpu.SemaphoreType.DMA((half + 1,)),
        ],
        compiler_params=pltpu.CompilerParams(
            collective_id=0, has_side_effects=True, vmem_limit_bytes=48 * 1024 * 1024
        ),
    )(mode_table(total), step_table(total), mode_pos, mode_vel, charges[None])


def solution(mesh):
    placed = (P("bead", None, "dom"), P("bead", None, "dom"), P("dom"))
    return jax.shard_map(
        local,
        mesh=mesh,
        in_specs=placed,
        out_specs=(P("bead", None, "dom"), P("bead", None, "dom")),
        check_vma=False,
    )
```

time: 85.4 us -> 57 us (0.67)
  blocking collectives: 27.4 us -> 0 us
  local copies, waits for them, and re-layouts: 2.05 us -> 3.43 us
  other arithmetic: 1.19 us -> 0 us
    all_gather x2 -> x0, blocking collectives: 27.4 us -> none  [the longest x1 16.5 us: local(): far = lax.all_gather(packed, 'dom', axis=0)]
    pallas_call x0 -> x2, local copies, waits for them, and re-layouts: none -> 1.25 us  [local(): pl.pallas_call(functools.partial(kernel, n_bead, n_dom), out_shape=(shape...]
    add x1 -> x0, other arithmetic: 0.86 us -> none  [evolve(): new_pos = cosine * mode_pos + carry_rate * mode_vel]
where the time goes in v2:
time: 57 us; the launch traced here: 56.8 us
  Pallas kernels  52.7 us (92%)
  local copies, waits for them, and re-layouts  3.43 us (6%)
  between operations  0.67 us (1%)
    pallas_call x1, Pallas kernels, local(): pl.pallas_call(functools.partial(kernel, n_bead, n_dom), out_shape=(shape...  52.7 us
    unnamed x8, local copies, waits for them, and re-layouts  1.48 us
    pallas_call x2, local copies, waits for them, and re-layouts, local(): pl.pallas_call(functools.partial(kernel, n_bead, n_dom), out_shape=(shape...  1.25 us

profile of v2, /device:TPU:0, one launch (start us, length us, event | category | flops | bytes accessed | tf_op | source)
XLA Modules:
  0.0 56.8 jit_solution(9221084966541802626)
XLA Ops:
  0.6 0.7 %broadcast_in_dim.3.charge_ref = f32[1,768]{1,0:T(1,128)S(1)} reshape(f32[768]{0:T(1024)} %param.7) | data formatting | bytes 6144 | tf_op jit(solution)/shard_map/broadcast_in_dim | solution.py:305
  1.3 0.0 copy-start.2
  1.3 0.8 %copy.7.pos_ref = f32[4,3,768]{2,1,0:T(4,128)S(1)} copy(f32[4,3,768]{2,0,1:T(4,128)} %param.5) | data formatting | bytes 73728 | tf_op args[0]
  2.1 0.0 copy-done.2
  2.1 0.0 copy-start
  2.1 0.0 copy-start.1
  2.2 0.7 %copy-done = f32[16,3]{1,0:T(8,128)S(1)} copy-done((f32[16,3]{1,0:T(8,128)S(1)}, f32[16,3]{1,0:T(8,128)}, u32[]{:S(2)}) %copy-start) | copy-done | bytes 216
  2.8 0.0 copy-done.1
  2.8 52.7 %shard_map.68 = (f32[4,3,768]{2,1,0:T(4,128)S(1)}, f32[4,3,768]{2,1,0:T(4,128)S(1)}) custom-call(f32[16,16]{1,0:T(8,128)S(1)} %copy-done.1, f32[16,3]{1,0:T(8,128)S(1)} %copy-done, f32[4,3,768]{2,1,0:T(4,128)S(1)} %copy.7.pos_ref, f32[4,3,768]{2,1,0:T(4,128)S(1)} %copy.8.vel_ref, f32[1,768]{1,0:T(1,128)S(1)} %broadcast_in_dim.3.charge_ref), custom_call_target="tpu_custom_call" | custom-call | tf_op jit(solution)/shard_map/pallas_call | solution.py:280
  55.5 0.6 %copy.9 = f32[4,3,768]{2,0,1:T(4,128)} copy(f32[4,3,768]{2,1,0:T(4,128)S(1)} %get-tuple-element.2) | data formatting | bytes 73728 | tf_op jit(solution)/shard_map/pallas_call | solution.py:280
  56.2 0.6 %copy.10 = f32[4,3,768]{2,0,1:T(4,128)} copy(f32[4,3,768]{2,1,0:T(4,128)S(1)} %get-tuple-element.3) | data formatting | bytes 73728 | tf_op jit(solution)/shard_map/pallas_call | solution.py:280
  (1 shorter events, 0.0 us)
Async XLA Ops:
  1.3 0.8 %copy-start.2 = (f32[4,3,768]{2,0,1:T(4,128)S(1)}, f32[4,3,768]{2,0,1:T(4,128)}, u32[]{:S(2)}) copy-start(f32[4,3,768]{2,0,1:T(4,128)} %param.6) | copy-start | bytes 110596
  2.1 0.7 %copy-start = (f32[16,3]{1,0:T(8,128)S(1)}, f32[16,3]{1,0:T(8,128)}, u32[]{:S(2)}) copy-start(f32[16,3]{1,0:T(8,128)} %constant.5.clone.step_ref) | copy-start | bytes 580
  2.1 0.7 %copy-start.1 = (f32[16,16]{1,0:T(8,128)S(1)}, f32[16,16]{1,0:T(8,128)}, u32[]{:S(2)}) copy-start(f32[16,16]{1,0:T(8,128)} %constant.4.clone.table_ref) | copy-start | bytes 3076

commit v3 on v2

--- a/solution.py
+++ b/solution.py
@@ -15,6 +15,7 @@
 STEP_TIME = 0.1
 LOG2E = 1.4426950408889634
 ROWS = 256
+STRIP = 16
 MESH = pl.DeviceIdType.MESH
 
 
@@ -91,21 +92,28 @@
     return decay * (1.0 + inverse) * (inverse * inverse)
 
 
-def block_sums(left, right, near, near_moment):
+def block_sums(left, right, near, near_moment, squares, weights):
+    far_count, count = squares.shape
     total, backs = None, []
-    for start in range(0, left.shape[0], ROWS):
-        square = jnp.dot(left[start : start + ROWS], near, preferred_element_type=jnp.float32)
-        weight = pair_weight(square)
-        high = weight.astype(jnp.bfloat16)
-        low = (weight - high.astype(jnp.float32)).astype(jnp.bfloat16)
+    for start in range(0, far_count, ROWS):
+        squares[start : start + ROWS] = jnp.dot(
+            left[start : start + ROWS], near, preferred_element_type=jnp.float32
+        )
+    for start in range(0, far_count, ROWS):
+        for strip in range(start, start + ROWS, STRIP):
+            weight = pair_weight(squares[strip : strip + STRIP])
+            high = weight.astype(jnp.bfloat16)
+            low = (weight - high.astype(jnp.float32)).astype(jnp.bfloat16)
+            weights[strip : strip + STRIP, :count] = high
+            weights[strip : strip + STRIP, count:] = low
         moment = right[:, start : start + ROWS]
+        high, low = weights[start : start + ROWS, :count], weights[start : start + ROWS, count:]
         part = jnp.dot(moment, high, preferred_element_type=jnp.float32)
         part += jnp.dot(moment, low, preferred_element_type=jnp.float32)
         total = part if total is None else total + part
         if near_moment is not None:
-            back = jnp.dot(high, near_moment, preferred_element_type=jnp.float32)
-            back += jnp.dot(low, near_moment, preferred_element_type=jnp.float32)
-            backs.append(back)
+            both = weights[start : start + ROWS]
+            backs.append(jnp.dot(both, near_moment, preferred_element_type=jnp.float32))
     back = jnp.concatenate(backs, axis=0).T if backs else None
     return total, back
 
@@ -117,7 +125,7 @@
 
 def kernel(
     n_bead, n_dom, table_ref, step_ref, pos_ref, vel_ref, charge_ref, pos_out, vel_out,
-    modes, packs, speed, centres, near_ops, near_moments, sums, backs, returned,
+    modes, packs, speed, centres, near_ops, near_moments, sums, backs, returned, squares, weights,
     mode_send, mode_recv, pack_send, pack_recv, back_send, back_recv,
 ):
     me_bead, me = lax.axis_index("bead"), lax.axis_index("dom")
@@ -184,7 +192,8 @@
         centres[b] = centre
         pos = scaled(pack, centre)
         near_ops[b] = near_operand(pos)
-        near_moments[b] = moment_parts(pos, charge).T.astype(jnp.bfloat16)
+        moment = moment_parts(pos, charge).T.astype(jnp.bfloat16)
+        near_moments[b] = jnp.concatenate((moment, moment), axis=0)
         sums[b] = jnp.zeros((32, tile[1]), jnp.float32)
 
     def one_unit(step, b, with_back):
@@ -192,7 +201,9 @@
         pos = scaled(pack, centres[b])
         right = moment_parts(pos, pack[3:4]).astype(jnp.bfloat16)
         moment = near_moments[b] if with_back else None
-        total, back = block_sums(far_operand(pos), right, near_ops[b], moment)
+        total, back = block_sums(
+            far_operand(pos), right, near_ops[b], moment, squares, weights
+        )
         sums[b] += total
         if with_back:
             backs[step, b] = force_of(pos, pack[3:4], back)
@@ -288,10 +299,12 @@
             pltpu.VMEM((beads, 8, count), jnp.float32),
             pltpu.VMEM((beads, 8, count), jnp.float32),
             pltpu.VMEM((beads, 48, count), jnp.bfloat16),
-            pltpu.VMEM((beads, count, 32), jnp.bfloat16),
+            pltpu.VMEM((beads, 2 * count, 32), jnp.bfloat16),
             pltpu.VMEM((beads, 32, count), jnp.float32),
             pltpu.VMEM((half + 1, beads, 8, count), jnp.float32),
             pltpu.VMEM((half + 1, beads, 8, count), jnp.float32),
+            pltpu.VMEM((count, count), jnp.float32),
+            pltpu.VMEM((count, 2 * count), jnp.bfloat16),
             pltpu.SemaphoreType.DMA((n_bead,)),
             pltpu.SemaphoreType.DMA((n_bead,)),
             pltpu.SemaphoreType.DMA((half + 1,)),

time: 57 us -> 49.5 us (0.87)
  Pallas kernels: 52.7 us -> 45.2 us
    pallas_call x1, Pallas kernels: 52.7 us -> 45.2 us  [local(): pl.pallas_call(functools.partial(kernel, n_bead, n_dom), out_shape=(shape...]
where the time goes in v3:
time: 49.5 us; the launch traced here: 49.3 us
  Pallas kernels  45.2 us (91%)
  local copies, waits for them, and re-layouts  3.43 us (7%)
  between operations  0.67 us (1%)
    pallas_call x1, Pallas kernels, local(): pl.pallas_call(functools.partial(kernel, n_bead, n_dom), out_shape=(shape...  45.2 us
    unnamed x8, local copies, waits for them, and re-layouts  1.48 us
    pallas_call x2, local copies, waits for them, and re-layouts, local(): pl.pallas_call(functools.partial(kernel, n_bead, n_dom), out_shape=(shape...  1.25 us

profile of v3, /device:TPU:0, one launch (start us, length us, event | category | flops | bytes accessed | tf_op | source)
XLA Modules:
  0.0 49.3 jit_solution(18335005036836835342)
XLA Ops:
  0.6 0.7 %broadcast_in_dim.3.charge_ref = f32[1,768]{1,0:T(1,128)S(1)} reshape(f32[768]{0:T(1024)} %param.7) | data formatting | bytes 6144 | tf_op jit(solution)/shard_map/broadcast_in_dim | solution.py:318
  1.3 0.0 copy-start.2
  1.3 0.8 %copy.7.pos_ref = f32[4,3,768]{2,1,0:T(4,128)S(1)} copy(f32[4,3,768]{2,0,1:T(4,128)} %param.5) | data formatting | bytes 73728 | tf_op args[0]
  2.1 0.0 copy-done.2
  2.1 0.0 copy-start
  2.1 0.0 copy-start.1
  2.2 0.7 %copy-done = f32[16,3]{1,0:T(8,128)S(1)} copy-done((f32[16,3]{1,0:T(8,128)S(1)}, f32[16,3]{1,0:T(8,128)}, u32[]{:S(2)}) %copy-start) | copy-done | bytes 216
  2.8 0.0 copy-done.1
  2.8 45.2 %shard_map.68 = (f32[4,3,768]{2,1,0:T(4,128)S(1)}, f32[4,3,768]{2,1,0:T(4,128)S(1)}) custom-call(f32[16,16]{1,0:T(8,128)S(1)} %copy-done.1, f32[16,3]{1,0:T(8,128)S(1)} %copy-done, f32[4,3,768]{2,1,0:T(4,128)S(1)} %copy.7.pos_ref, f32[4,3,768]{2,1,0:T(4,128)S(1)} %copy.8.vel_ref, f32[1,768]{1,0:T(1,128)S(1)} %broadcast_in_dim.3.charge_ref), custom_call_target="tpu_custom_call" | custom-call | tf_op jit(solution)/shard_map/pallas_call | solution.py:291
  48.0 0.6 %copy.9 = f32[4,3,768]{2,0,1:T(4,128)} copy(f32[4,3,768]{2,1,0:T(4,128)S(1)} %get-tuple-element.2) | data formatting | bytes 73728 | tf_op jit(solution)/shard_map/pallas_call | solution.py:291
  48.6 0.6 %copy.10 = f32[4,3,768]{2,0,1:T(4,128)} copy(f32[4,3,768]{2,1,0:T(4,128)S(1)} %get-tuple-element.3) | data formatting | bytes 73728 | tf_op jit(solution)/shard_map/pallas_call | solution.py:291
  (1 shorter events, 0.0 us)
Async XLA Ops:
  1.3 0.8 %copy-start.2 = (f32[4,3,768]{2,0,1:T(4,128)S(1)}, f32[4,3,768]{2,0,1:T(4,128)}, u32[]{:S(2)}) copy-start(f32[4,3,768]{2,0,1:T(4,128)} %param.6) | copy-start | bytes 110596
  2.1 0.7 %copy-start = (f32[16,3]{1,0:T(8,128)S(1)}, f32[16,3]{1,0:T(8,128)}, u32[]{:S(2)}) copy-start(f32[16,3]{1,0:T(8,128)} %constant.5.clone.step_ref) | copy-start | bytes 580
  2.1 0.7 %copy-start.1 = (f32[16,16]{1,0:T(8,128)S(1)}, f32[16,16]{1,0:T(8,128)}, u32[]{:S(2)}) copy-start(f32[16,16]{1,0:T(8,128)} %constant.4.clone.table_ref) | copy-start | bytes 3076

commit v4 on v2

--- a/solution.py
+++ b/solution.py
@@ -15,6 +15,7 @@
 STEP_TIME = 0.1
 LOG2E = 1.4426950408889634
 ROWS = 256
+STRIP = 16
 MESH = pl.DeviceIdType.MESH
 
 
@@ -91,23 +92,31 @@
     return decay * (1.0 + inverse) * (inverse * inverse)
 
 
-def block_sums(left, right, near, near_moment):
-    total, backs = None, []
-    for start in range(0, left.shape[0], ROWS):
-        square = jnp.dot(left[start : start + ROWS], near, preferred_element_type=jnp.float32)
-        weight = pair_weight(square)
+def square_rows(start, left, near, squares):
+    rows = pl.ds(start, ROWS)
+    squares[rows] = jnp.dot(left[rows], near[...], preferred_element_type=jnp.float32)
+
+
+def weigh_rows(start, squares, weights):
+    count = squares.shape[1]
+    for strip in range(start, start + ROWS, STRIP):
+        weight = pair_weight(squares[strip : strip + STRIP])
         high = weight.astype(jnp.bfloat16)
         low = (weight - high.astype(jnp.float32)).astype(jnp.bfloat16)
-        moment = right[:, start : start + ROWS]
-        part = jnp.dot(moment, high, preferred_element_type=jnp.float32)
-        part += jnp.dot(moment, low, preferred_element_type=jnp.float32)
-        total = part if total is None else total + part
-        if near_moment is not None:
-            back = jnp.dot(high, near_moment, preferred_element_type=jnp.float32)
-            back += jnp.dot(low, near_moment, preferred_element_type=jnp.float32)
-            backs.append(back)
-    back = jnp.concatenate(backs, axis=0).T if backs else None
-    return total, back
+        weights[strip : strip + STRIP, :count] = high
+        weights[strip : strip + STRIP, count:] = low
+
+
+def near_sums(start, right, weights):
+    rows, count = pl.ds(start, ROWS), weights.shape[1] // 2
+    moment = right[:, rows]
+    high = jnp.dot(moment, weights[rows, :count], preferred_element_type=jnp.float32)
+    return high + jnp.dot(moment, weights[rows, count:], preferred_element_type=jnp.float32)
+
+
+def far_sums(start, near_moment, weights, back):
+    rows = pl.ds(start, ROWS)
+    back[rows] = jnp.dot(weights[rows], near_moment[...], preferred_element_type=jnp.float32)
 
 
 def force_of(pos, charge, sums):
@@ -117,12 +126,13 @@
 
 def kernel(
     n_bead, n_dom, table_ref, step_ref, pos_ref, vel_ref, charge_ref, pos_out, vel_out,
-    modes, packs, speed, centres, near_ops, near_moments, sums, backs, returned,
-    mode_send, mode_recv, pack_send, pack_recv, back_send, back_recv,
+    modes, packs, speed, centres, near_ops, near_moments, sums, backs, returned, squares, weights,
+    lefts, rights, raw_backs, mode_send, mode_recv, pack_send, pack_recv, back_send, back_recv,
 ):
     me_bead, me = lax.axis_index("bead"), lax.axis_index("dom")
     beads, half = pos_ref.shape[0], n_dom // 2
     part = beads // 2
+    group = squares.shape[0]
     tile = (8, pos_ref.shape[2])
     row = row_index(tile)
 
@@ -184,21 +194,35 @@
         centres[b] = centre
         pos = scaled(pack, centre)
         near_ops[b] = near_operand(pos)
-        near_moments[b] = moment_parts(pos, charge).T.astype(jnp.bfloat16)
+        moment = moment_parts(pos, charge).T.astype(jnp.bfloat16)
+        near_moments[b] = jnp.concatenate((moment, moment), axis=0)
         sums[b] = jnp.zeros((32, tile[1]), jnp.float32)
 
-    def one_unit(step, b, with_back):
-        pack = packs[step, b]
-        pos = scaled(pack, centres[b])
-        right = moment_parts(pos, pack[3:4]).astype(jnp.bfloat16)
-        moment = near_moments[b] if with_back else None
-        total, back = block_sums(far_operand(pos), right, near_ops[b], moment)
-        sums[b] += total
-        if with_back:
-            backs[step, b] = force_of(pos, pack[3:4], back)
-
-    def own_unit(b, unused):
-        one_unit(0, b, False)
+    def prepare(step):
+        for b in range(beads):
+            pack = packs[step, b]
+            pos = scaled(pack, centres[b])
+            lefts[b] = far_operand(pos)
+            rights[b] = moment_parts(pos, pack[3:4]).astype(jnp.bfloat16)
+
+    def some_beads(first, with_back):
+        starts = range(0, tile[1], ROWS)
+        for start in starts:
+            square_rows(start, lefts.at[first], near_ops.at[first], squares.at[0])
+        for i in range(group):
+            b = first + i
+            total = sums[b]
+            for start in starts:
+                weigh_rows(start, squares.at[i], weights.at[i])
+                if i + 1 < group:
+                    square_rows(start, lefts.at[b + 1], near_ops.at[b + 1], squares.at[i + 1])
+                total += near_sums(start, rights.at[b], weights.at[i])
+                if with_back:
+                    far_sums(start, near_moments.at[b], weights.at[i], raw_backs.at[b])
+            sums[b] = total
+
+    def own_beads(g, unused):
+        some_beads(g * group, False)
         return unused
 
     mine = jnp.where(me < half, 0, part)
@@ -220,18 +244,23 @@
             device_id={"dom": lax.rem(me - half + n_dom, n_dom)}, device_id_type=MESH,
         )
 
-    lax.fori_loop(0, part, own_unit, 0)
+    prepare(0)
+    lax.fori_loop(0, part // group, own_beads, 0)
 
     def one_step(step, unused):
         pack_copy(step).wait_recv()
+        prepare(step)
         first = jnp.where(step < half, 0, mine)
-        count = jnp.where(step < half, beads, part)
-
-        def unit(b, inner):
-            one_unit(step, first + b, True)
+        count = jnp.where(step < half, beads // group, part // group)
+
+        def unit(g, inner):
+            some_beads(first + g * group, True)
             return inner
 
         lax.fori_loop(0, count, unit, 0)
+        for b in range(beads):
+            pack = packs[step, b]
+            backs[step, b] = force_of(scaled(pack, centres[b]), pack[3:4], raw_backs[b].T)
 
         @pl.when(step < half)
         def _():
@@ -241,7 +270,8 @@
 
     lax.fori_loop(1, half + 1, one_step, 0)
     last_copy(mine).start()
-    lax.fori_loop(part, beads, own_unit, 0)
+    prepare(0)
+    lax.fori_loop(part // group, beads // group, own_beads, 0)
 
     for b in range(beads):
         pack = packs[0, b]
@@ -275,6 +305,7 @@
     beads, unused, count = mode_pos.shape
     half = n_dom // 2
     total = n_bead * beads
+    group = 2 if beads % 4 == 0 else 1
     vmem, smem = pl.BlockSpec(memory_space=pltpu.VMEM), pl.BlockSpec(memory_space=pltpu.SMEM)
     shape = jax.ShapeDtypeStruct(mode_pos.shape, jnp.float32)
     return pl.pallas_call(
@@ -288,10 +319,15 @@
             pltpu.VMEM((beads, 8, count), jnp.float32),
             pltpu.VMEM((beads, 8, count), jnp.float32),
             pltpu.VMEM((beads, 48, count), jnp.bfloat16),
-            pltpu.VMEM((beads, count, 32), jnp.bfloat16),
+            pltpu.VMEM((beads, 2 * count, 32), jnp.bfloat16),
             pltpu.VMEM((beads, 32, count), jnp.float32),
             pltpu.VMEM((half + 1, beads, 8, count), jnp.float32),
             pltpu.VMEM((half + 1, beads, 8, count), jnp.float32),
+            pltpu.VMEM((group, count, count), jnp.float32),
+            pltpu.VMEM((group, count, 2 * count), jnp.bfloat16),
+            pltpu.VMEM((beads, count, 48), jnp.bfloat16),
+            pltpu.VMEM((beads, 32, count), jnp.bfloat16),
+            pltpu.VMEM((beads, count, 32), jnp.float32),
             pltpu.SemaphoreType.DMA((n_bead,)),
             pltpu.SemaphoreType.DMA((n_bead,)),
             pltpu.SemaphoreType.DMA((half + 1,)),

time: 57 us -> 48.5 us (0.85)
  Pallas kernels: 52.7 us -> 44.2 us
    pallas_call x1, Pallas kernels: 52.7 us -> 44.2 us  [local(): pl.pallas_call(functools.partial(kernel, n_bead, n_dom), out_shape=(shape...]
where the time goes in v4:
time: 48.5 us; the launch traced here: 48.3 us
  Pallas kernels  44.2 us (91%)
  local copies, waits for them, and re-layouts  3.43 us (7%)
  between operations  0.67 us (1%)
    pallas_call x1, Pallas kernels, local(): pl.pallas_call(functools.partial(kernel, n_bead, n_dom), out_shape=(shape...  44.2 us
    unnamed x8, local copies, waits for them, and re-layouts  1.48 us
    pallas_call x2, local copies, waits for them, and re-layouts, local(): pl.pallas_call(functools.partial(kernel, n_bead, n_dom), out_shape=(shape...  1.25 us

profile of v4, /device:TPU:0, one launch (start us, length us, event | category | flops | bytes accessed | tf_op | source)
XLA Modules:
  0.0 48.3 jit_solution(9344747230773737672)
XLA Ops:
  0.6 0.7 %broadcast_in_dim.3.charge_ref = f32[1,768]{1,0:T(1,128)S(1)} reshape(f32[768]{0:T(1024)} %param.7) | data formatting | bytes 6144 | tf_op jit(solution)/shard_map/broadcast_in_dim | solution.py:341
  1.3 0.0 copy-start.2
  1.3 0.8 %copy.7.pos_ref = f32[4,3,768]{2,1,0:T(4,128)S(1)} copy(f32[4,3,768]{2,0,1:T(4,128)} %param.5) | data formatting | bytes 73728 | tf_op args[0]
  2.1 0.0 copy-done.2
  2.1 0.0 copy-start
  2.1 0.0 copy-start.1
  2.2 0.7 %copy-done = f32[16,3]{1,0:T(8,128)S(1)} copy-done((f32[16,3]{1,0:T(8,128)S(1)}, f32[16,3]{1,0:T(8,128)}, u32[]{:S(2)}) %copy-start) | copy-done | bytes 216
  2.8 0.0 copy-done.1
  2.8 44.2 %shard_map.68 = (f32[4,3,768]{2,1,0:T(4,128)S(1)}, f32[4,3,768]{2,1,0:T(4,128)S(1)}) custom-call(f32[16,16]{1,0:T(8,128)S(1)} %copy-done.1, f32[16,3]{1,0:T(8,128)S(1)} %copy-done, f32[4,3,768]{2,1,0:T(4,128)S(1)} %copy.7.pos_ref, f32[4,3,768]{2,1,0:T(4,128)S(1)} %copy.8.vel_ref, f32[1,768]{1,0:T(1,128)S(1)} %broadcast_in_dim.3.charge_ref), custom_call_target="tpu_custom_call" | custom-call | tf_op jit(solution)/shard_map/pallas_call | solution.py:311
  47.0 0.6 %copy.9 = f32[4,3,768]{2,0,1:T(4,128)} copy(f32[4,3,768]{2,1,0:T(4,128)S(1)} %get-tuple-element.2) | data formatting | bytes 73728 | tf_op jit(solution)/shard_map/pallas_call | solution.py:311
  47.7 0.6 %copy.10 = f32[4,3,768]{2,0,1:T(4,128)} copy(f32[4,3,768]{2,1,0:T(4,128)S(1)} %get-tuple-element.3) | data formatting | bytes 73728 | tf_op jit(solution)/shard_map/pallas_call | solution.py:311
  (1 shorter events, 0.0 us)
Async XLA Ops:
  1.3 0.8 %copy-start.2 = (f32[4,3,768]{2,0,1:T(4,128)S(1)}, f32[4,3,768]{2,0,1:T(4,128)}, u32[]{:S(2)}) copy-start(f32[4,3,768]{2,0,1:T(4,128)} %param.6) | copy-start | bytes 110596
  2.1 0.7 %copy-start = (f32[16,3]{1,0:T(8,128)S(1)}, f32[16,3]{1,0:T(8,128)}, u32[]{:S(2)}) copy-start(f32[16,3]{1,0:T(8,128)} %constant.5.clone.step_ref) | copy-start | bytes 580
  2.1 0.7 %copy-start.1 = (f32[16,16]{1,0:T(8,128)S(1)}, f32[16,16]{1,0:T(8,128)}, u32[]{:S(2)}) copy-start(f32[16,16]{1,0:T(8,128)} %constant.4.clone.table_ref) | copy-start | bytes 3076

commit v5 on v4

--- a/solution.py
+++ b/solution.py
@@ -92,9 +92,8 @@
     return decay * (1.0 + inverse) * (inverse * inverse)
 
 
-def square_rows(start, left, near, squares):
-    rows = pl.ds(start, ROWS)
-    squares[rows] = jnp.dot(left[rows], near[...], preferred_element_type=jnp.float32)
+def square_rows(left, near, squares):
+    squares[...] = jnp.dot(left[...], near[...], preferred_element_type=jnp.float32)
 
 
 def weigh_rows(start, squares, weights):
@@ -114,9 +113,8 @@
     return high + jnp.dot(moment, weights[rows, count:], preferred_element_type=jnp.float32)
 
 
-def far_sums(start, near_moment, weights, back):
-    rows = pl.ds(start, ROWS)
-    back[rows] = jnp.dot(weights[rows], near_moment[...], preferred_element_type=jnp.float32)
+def far_sums(near_moment, weights, back):
+    back[...] = jnp.dot(weights[...], near_moment[...], preferred_element_type=jnp.float32)
 
 
 def force_of(pos, charge, sums):
@@ -206,20 +204,18 @@
             rights[b] = moment_parts(pos, pack[3:4]).astype(jnp.bfloat16)
 
     def some_beads(first, with_back):
-        starts = range(0, tile[1], ROWS)
-        for start in starts:
-            square_rows(start, lefts.at[first], near_ops.at[first], squares.at[0])
+        square_rows(lefts.at[first], near_ops.at[first], squares.at[0])
         for i in range(group):
             b = first + i
             total = sums[b]
-            for start in starts:
+            for start in range(0, tile[1], ROWS):
                 weigh_rows(start, squares.at[i], weights.at[i])
-                if i + 1 < group:
-                    square_rows(start, lefts.at[b + 1], near_ops.at[b + 1], squares.at[i + 1])
+                if start == 0 and i + 1 < group:
+                    square_rows(lefts.at[b + 1], near_ops.at[b + 1], squares.at[i + 1])
                 total += near_sums(start, rights.at[b], weights.at[i])
-                if with_back:
-                    far_sums(start, near_moments.at[b], weights.at[i], raw_backs.at[b])
             sums[b] = total
+            if with_back:
+                far_sums(near_moments.at[b], weights.at[i], raw_backs.at[b])
 
     def own_beads(g, unused):
         some_beads(g * group, False)

time: 48.5 us -> 52.7 us (1.087)
  Pallas kernels: 44.2 us -> 48.4 us
    pallas_call x1, Pallas kernels: 44.2 us -> 48.4 us  [local(): pl.pallas_call(functools.partial(kernel, n_bead, n_dom), out_shape=(shape...]
where the time goes in v5:
time: 52.7 us; the launch traced here: 52.5 us
  Pallas kernels  48.4 us (92%)
  local copies, waits for them, and re-layouts  3.43 us (7%)
  between operations  0.67 us (1%)
    pallas_call x1, Pallas kernels, local(): pl.pallas_call(functools.partial(kernel, n_bead, n_dom), out_shape=(shape...  48.4 us
    unnamed x8, local copies, waits for them, and re-layouts  1.48 us
    pallas_call x2, local copies, waits for them, and re-layouts, local(): pl.pallas_call(functools.partial(kernel, n_bead, n_dom), out_shape=(shape...  1.25 us

profile of v5, /device:TPU:0, one launch (start us, length us, event | category | flops | bytes accessed | tf_op | source)
XLA Modules:
  0.0 52.5 jit_solution(5968061627470999108)
XLA Ops:
  0.6 0.7 %broadcast_in_dim.3.charge_ref = f32[1,768]{1,0:T(1,128)S(1)} reshape(f32[768]{0:T(1024)} %param.7) | data formatting | bytes 6144 | tf_op jit(solution)/shard_map/broadcast_in_dim | solution.py:337
  1.3 0.0 copy-start.2
  1.3 0.8 %copy.7.pos_ref = f32[4,3,768]{2,1,0:T(4,128)S(1)} copy(f32[4,3,768]{2,0,1:T(4,128)} %param.5) | data formatting | bytes 73728 | tf_op args[0]
  2.1 0.0 copy-done.2
  2.1 0.0 copy-start
  2.1 0.0 copy-start.1
  2.2 0.7 %copy-done = f32[16,3]{1,0:T(8,128)S(1)} copy-done((f32[16,3]{1,0:T(8,128)S(1)}, f32[16,3]{1,0:T(8,128)}, u32[]{:S(2)}) %copy-start) | copy-done | bytes 216
  2.8 0.0 copy-done.1
  2.8 48.4 %shard_map.68 = (f32[4,3,768]{2,1,0:T(4,128)S(1)}, f32[4,3,768]{2,1,0:T(4,128)S(1)}) custom-call(f32[16,16]{1,0:T(8,128)S(1)} %copy-done.1, f32[16,3]{1,0:T(8,128)S(1)} %copy-done, f32[4,3,768]{2,1,0:T(4,128)S(1)} %copy.7.pos_ref, f32[4,3,768]{2,1,0:T(4,128)S(1)} %copy.8.vel_ref, f32[1,768]{1,0:T(1,128)S(1)} %broadcast_in_dim.3.charge_ref), custom_call_target="tpu_custom_call" | custom-call | tf_op jit(solution)/shard_map/pallas_call | solution.py:307
  51.2 0.6 %copy.9 = f32[4,3,768]{2,0,1:T(4,128)} copy(f32[4,3,768]{2,1,0:T(4,128)S(1)} %get-tuple-element.2) | data formatting | bytes 73728 | tf_op jit(solution)/shard_map/pallas_call | solution.py:307
  51.8 0.6 %copy.10 = f32[4,3,768]{2,0,1:T(4,128)} copy(f32[4,3,768]{2,1,0:T(4,128)S(1)} %get-tuple-element.3) | data formatting | bytes 73728 | tf_op jit(solution)/shard_map/pallas_call | solution.py:307
  (1 shorter events, 0.0 us)
Async XLA Ops:
  1.3 0.8 %copy-start.2 = (f32[4,3,768]{2,0,1:T(4,128)S(1)}, f32[4,3,768]{2,0,1:T(4,128)}, u32[]{:S(2)}) copy-start(f32[4,3,768]{2,0,1:T(4,128)} %param.6) | copy-start | bytes 110596
  2.1 0.7 %copy-start = (f32[16,3]{1,0:T(8,128)S(1)}, f32[16,3]{1,0:T(8,128)}, u32[]{:S(2)}) copy-start(f32[16,3]{1,0:T(8,128)} %constant.5.clone.step_ref) | copy-start | bytes 580
  2.1 0.7 %copy-start.1 = (f32[16,16]{1,0:T(8,128)S(1)}, f32[16,16]{1,0:T(8,128)}, u32[]{:S(2)}) copy-start(f32[16,16]{1,0:T(8,128)} %constant.4.clone.table_ref) | copy-start | bytes 3076

commit v6 on v5

--- a/solution.py
+++ b/solution.py
@@ -16,6 +16,7 @@
 LOG2E = 1.4426950408889634
 ROWS = 256
 STRIP = 16
+LANES = 256
 MESH = pl.DeviceIdType.MESH
 
 
@@ -92,29 +93,47 @@
     return decay * (1.0 + inverse) * (inverse * inverse)
 
 
-def square_rows(left, near, squares):
-    squares[...] = jnp.dot(left[...], near[...], preferred_element_type=jnp.float32)
-
-
-def weigh_rows(start, squares, weights):
+def square_pieces(start, left, near, squares):
+    rows = pl.ds(start, ROWS)
+
+    def piece(lanes):
+        squares[rows, lanes] = jnp.dot(
+            left[rows], near[:, lanes], preferred_element_type=jnp.float32
+        )
+
+    return [functools.partial(piece, lanes) for lanes in lane_tiles(squares.shape[1])]
+
+
+def lane_tiles(count):
+    return [pl.ds(lane, LANES) for lane in range(0, count, LANES)]
+
+
+def weigh_strip(strip, squares, weights):
     count = squares.shape[1]
-    for strip in range(start, start + ROWS, STRIP):
-        weight = pair_weight(squares[strip : strip + STRIP])
-        high = weight.astype(jnp.bfloat16)
-        low = (weight - high.astype(jnp.float32)).astype(jnp.bfloat16)
-        weights[strip : strip + STRIP, :count] = high
-        weights[strip : strip + STRIP, count:] = low
-
-
-def near_sums(start, right, weights):
+    weight = pair_weight(squares[strip : strip + STRIP])
+    high = weight.astype(jnp.bfloat16)
+    low = (weight - high.astype(jnp.float32)).astype(jnp.bfloat16)
+    weights[strip : strip + STRIP, :count] = high
+    weights[strip : strip + STRIP, count:] = low
+
+
+def near_pieces(start, right, weights, sums):
     rows, count = pl.ds(start, ROWS), weights.shape[1] // 2
-    moment = right[:, rows]
-    high = jnp.dot(moment, weights[rows, :count], preferred_element_type=jnp.float32)
-    return high + jnp.dot(moment, weights[rows, count:], preferred_element_type=jnp.float32)
-
-
-def far_sums(near_moment, weights, back):
-    back[...] = jnp.dot(weights[...], near_moment[...], preferred_element_type=jnp.float32)
+
+    def piece(lane):
+        moment = right[:, rows]
+        high = weights[rows, lane : lane + LANES]
+        low = weights[rows, count + lane : count + lane + LANES]
+        part = jnp.dot(moment, high, preferred_element_type=jnp.float32)
+        part += jnp.dot(moment, low, preferred_element_type=jnp.float32)
+        sums[:, lane : lane + LANES] += part
+
+    return [functools.partial(piece, lane) for lane in range(0, count, LANES)]
+
+
+def far_piece(start, near_moment, weights, back):
+    rows = pl.ds(start, ROWS)
+    back[rows] = jnp.dot(weights[rows], near_moment[...], preferred_element_type=jnp.float32)
 
 
 def force_of(pos, charge, sums):
@@ -204,18 +223,38 @@
             rights[b] = moment_parts(pos, pack[3:4]).astype(jnp.bfloat16)
 
     def some_beads(first, with_back):
-        square_rows(lefts.at[first], near_ops.at[first], squares.at[0])
-        for i in range(group):
+        chunks = [(i, start) for i in range(group) for start in range(0, tile[1], ROWS)]
+
+        def before(turn):
+            i, start = chunks[turn]
             b = first + i
-            total = sums[b]
-            for start in range(0, tile[1], ROWS):
-                weigh_rows(start, squares.at[i], weights.at[i])
-                if start == 0 and i + 1 < group:
-                    square_rows(lefts.at[b + 1], near_ops.at[b + 1], squares.at[i + 1])
-                total += near_sums(start, rights.at[b], weights.at[i])
-            sums[b] = total
+            return square_pieces(start, lefts.at[b], near_ops.at[b], squares.at[i])
+
+        def after(turn):
+            i, start = chunks[turn]
+            b = first + i
+            pieces = near_pieces(start, rights.at[b], weights.at[i], sums.at[b])
             if with_back:
-                far_sums(near_moments.at[b], weights.at[i], raw_backs.at[b])
+                one = functools.partial(
+                    far_piece, start, near_moments.at[b], weights.at[i], raw_backs.at[b]
+                )
+                pieces.insert(1, one)
+            return pieces
+
+        for piece in before(0):
+            piece()
+        for turn, (i, start) in enumerate(chunks):
+            pieces = after(turn - 1) if turn else []
+            pieces += before(turn + 1) if turn + 1 < len(chunks) else []
+            strips = list(range(start, start + ROWS, STRIP))
+            for n, strip in enumerate(strips):
+                weigh_strip(strip, squares.at[i], weights.at[i])
+                if pieces and n % 2 == 0:
+                    pieces.pop(0)()
+            for piece in pieces:
+                piece()
+        for piece in after(len(chunks) - 1):
+            piece()
 
     def own_beads(g, unused):
         some_beads(g * group, False)

time: 52.7 us -> 47.1 us (0.89)
  Pallas kernels: 48.4 us -> 42.8 us
    pallas_call x1, Pallas kernels: 48.4 us -> 42.8 us  [local(): pl.pallas_call(functools.partial(kernel, n_bead, n_dom), out_shape=(shape...]
where the time goes in v6:
time: 47.1 us; the launch traced here: 46.9 us
  Pallas kernels  42.8 us (91%)
  local copies, waits for them, and re-layouts  3.43 us (7%)
  between operations  0.67 us (1%)
    pallas_call x1, Pallas kernels, local(): pl.pallas_call(functools.partial(kernel, n_bead, n_dom), out_shape=(shape...  42.8 us
    unnamed x8, local copies, waits for them, and re-layouts  1.48 us
    pallas_call x2, local copies, waits for them, and re-layouts, local(): pl.pallas_call(functools.partial(kernel, n_bead, n_dom), out_shape=(shape...  1.25 us

profile of v6, /device:TPU:0, one launch (start us, length us, event | category | flops | bytes accessed | tf_op | source)
XLA Modules:
  0.0 46.9 jit_solution(12999274425118411062)
XLA Ops:
  0.6 0.7 %broadcast_in_dim.3.charge_ref = f32[1,768]{1,0:T(1,128)S(1)} reshape(f32[768]{0:T(1024)} %param.7) | data formatting | bytes 6144 | tf_op jit(solution)/shard_map/broadcast_in_dim | solution.py:376
  1.3 0.0 copy-start.2
  1.3 0.8 %copy.7.pos_ref = f32[4,3,768]{2,1,0:T(4,128)S(1)} copy(f32[4,3,768]{2,0,1:T(4,128)} %param.5) | data formatting | bytes 73728 | tf_op args[0]
  2.1 0.0 copy-done.2
  2.1 0.0 copy-start
  2.1 0.0 copy-start.1
  2.2 0.7 %copy-done = f32[16,3]{1,0:T(8,128)S(1)} copy-done((f32[16,3]{1,0:T(8,128)S(1)}, f32[16,3]{1,0:T(8,128)}, u32[]{:S(2)}) %copy-start) | copy-done | bytes 216
  2.8 0.0 copy-done.1
  2.8 42.8 %shard_map.68 = (f32[4,3,768]{2,1,0:T(4,128)S(1)}, f32[4,3,768]{2,1,0:T(4,128)S(1)}) custom-call(f32[16,16]{1,0:T(8,128)S(1)} %copy-done.1, f32[16,3]{1,0:T(8,128)S(1)} %copy-done, f32[4,3,768]{2,1,0:T(4,128)S(1)} %copy.7.pos_ref, f32[4,3,768]{2,1,0:T(4,128)S(1)} %copy.8.vel_ref, f32[1,768]{1,0:T(1,128)S(1)} %broadcast_in_dim.3.charge_ref), custom_call_target="tpu_custom_call" | custom-call | tf_op jit(solution)/shard_map/pallas_call | solution.py:346
  45.6 0.6 %copy.9 = f32[4,3,768]{2,0,1:T(4,128)} copy(f32[4,3,768]{2,1,0:T(4,128)S(1)} %get-tuple-element.2) | data formatting | bytes 73728 | tf_op jit(solution)/shard_map/pallas_call | solution.py:346
  46.3 0.6 %copy.10 = f32[4,3,768]{2,0,1:T(4,128)} copy(f32[4,3,768]{2,1,0:T(4,128)S(1)} %get-tuple-element.3) | data formatting | bytes 73728 | tf_op jit(solution)/shard_map/pallas_call | solution.py:346
  (1 shorter events, 0.0 us)
Async XLA Ops:
  1.3 0.8 %copy-start.2 = (f32[4,3,768]{2,0,1:T(4,128)S(1)}, f32[4,3,768]{2,0,1:T(4,128)}, u32[]{:S(2)}) copy-start(f32[4,3,768]{2,0,1:T(4,128)} %param.6) | copy-start | bytes 110596
  2.1 0.7 %copy-start = (f32[16,3]{1,0:T(8,128)S(1)}, f32[16,3]{1,0:T(8,128)}, u32[]{:S(2)}) copy-start(f32[16,3]{1,0:T(8,128)} %constant.5.clone.step_ref) | copy-start | bytes 580
  2.1 0.7 %copy-start.1 = (f32[16,16]{1,0:T(8,128)S(1)}, f32[16,16]{1,0:T(8,128)}, u32[]{:S(2)}) copy-start(f32[16,16]{1,0:T(8,128)} %constant.4.clone.table_ref) | copy-start | bytes 3076

commit v7 on v6

--- a/solution.py
+++ b/solution.py
@@ -133,7 +133,10 @@
 
 def far_piece(start, near_moment, weights, back):
     rows = pl.ds(start, ROWS)
-    back[rows] = jnp.dot(weights[rows], near_moment[...], preferred_element_type=jnp.float32)
+    back[:, rows] = lax.dot_general(
+        near_moment[...], weights[rows], (((1,), (1,)), ((), ())),
+        preferred_element_type=jnp.float32,
+    )
 
 
 def force_of(pos, charge, sums):
@@ -190,7 +193,7 @@
             for b in range(beads):
                 mixed[b] = mixed[b] + table_ref[me_bead * beads + b, first + k] * mode
 
-    charge = charge_ref[...]
+    charge = charge_ref[...].reshape(1, tile[1])
     for b in range(beads):
         packs[0, b] = jnp.where(row < 3, mixed[b], jnp.where(row == 3, charge, 0.0))
 
@@ -211,8 +214,8 @@
         centres[b] = centre
         pos = scaled(pack, centre)
         near_ops[b] = near_operand(pos)
-        moment = moment_parts(pos, charge).T.astype(jnp.bfloat16)
-        near_moments[b] = jnp.concatenate((moment, moment), axis=0)
+        moment = moment_parts(pos, charge).astype(jnp.bfloat16)
+        near_moments[b] = jnp.concatenate((moment, moment), axis=1)
         sums[b] = jnp.zeros((32, tile[1]), jnp.float32)
 
     def prepare(step):
@@ -295,7 +298,7 @@
         lax.fori_loop(0, count, unit, 0)
         for b in range(beads):
             pack = packs[step, b]
-            backs[step, b] = force_of(scaled(pack, centres[b]), pack[3:4], raw_backs[b].T)
+            backs[step, b] = force_of(scaled(pack, centres[b]), pack[3:4], raw_backs[b])
 
         @pl.when(step < half)
         def _():
@@ -354,7 +357,7 @@
             pltpu.VMEM((beads, 8, count), jnp.float32),
             pltpu.VMEM((beads, 8, count), jnp.float32),
             pltpu.VMEM((beads, 48, count), jnp.bfloat16),
-            pltpu.VMEM((beads, 2 * count, 32), jnp.bfloat16),
+            pltpu.VMEM((beads, 32, 2 * count), jnp.bfloat16),
             pltpu.VMEM((beads, 32, count), jnp.float32),
             pltpu.VMEM((half + 1, beads, 8, count), jnp.float32),
             pltpu.VMEM((half + 1, beads, 8, count), jnp.float32),
@@ -362,7 +365,7 @@
             pltpu.VMEM((group, count, 2 * count), jnp.bfloat16),
             pltpu.VMEM((beads, count, 48), jnp.bfloat16),
             pltpu.VMEM((beads, 32, count), jnp.bfloat16),
-            pltpu.VMEM((beads, count, 32), jnp.float32),
+            pltpu.VMEM((beads, 32, count), jnp.float32),
             pltpu.SemaphoreType.DMA((n_bead,)),
             pltpu.SemaphoreType.DMA((n_bead,)),
             pltpu.SemaphoreType.DMA((half + 1,)),
@@ -373,7 +376,7 @@
         compiler_params=pltpu.CompilerParams(
             collective_id=0, has_side_effects=True, vmem_limit_bytes=48 * 1024 * 1024
         ),
-    )(mode_table(total), step_table(total), mode_pos, mode_vel, charges[None])
+    )(mode_table(total), step_table(total), mode_pos, mode_vel, charges)
 
 
 def solution(mesh):

time: 47.1 us -> 44.8 us (0.951)
  Pallas kernels: 42.8 us -> 41.1 us
  local copies, waits for them, and re-layouts: 3.43 us -> 2.74 us
    pallas_call x1, Pallas kernels: 42.8 us -> 41.1 us  [local(): pl.pallas_call(functools.partial(kernel, n_bead, n_dom), out_shape=(shape...]
    broadcast_in_dim x1 -> x0, local copies, waits for them, and re-layouts: 0.69 us -> none  [local(): charges[None]]
    unnamed x8 -> x10, local copies, waits for them, and re-layouts: 1.48 us -> 1.48 us
where the time goes in v7:
time: 44.8 us; the launch traced here: 44.6 us
  Pallas kernels  41.1 us (92%)
  local copies, waits for them, and re-layouts  2.74 us (6%)
  between operations  0.69 us (2%)
    pallas_call x1, Pallas kernels, local(): pl.pallas_call(functools.partial(kernel, n_bead, n_dom), out_shape=(shape...  41.1 us
    unnamed x10, local copies, waits for them, and re-layouts  1.48 us
    pallas_call x2, local copies, waits for them, and re-layouts, local(): pl.pallas_call(functools.partial(kernel, n_bead, n_dom), out_shape=(shape...  1.25 us

profile of v7, /device:TPU:0, one launch (start us, length us, event | category | flops | bytes accessed | tf_op | source)
XLA Modules:
  0.0 44.6 jit_solution(13823770632874178002)
XLA Ops:
  0.6 0.0 copy-start.3
  0.6 0.8 %copy.7.pos_ref = f32[4,3,768]{2,1,0:T(4,128)S(1)} copy(f32[4,3,768]{2,0,1:T(4,128)} %param.5) | data formatting | bytes 73728 | tf_op args[0]
  1.4 0.0 copy-done.3
  1.4 0.0 copy-start
  1.5 0.0 copy-start.1
  1.5 0.0 copy-start.2
  1.5 0.6 %copy-done = f32[16,3]{1,0:T(8,128)S(1)} copy-done((f32[16,3]{1,0:T(8,128)S(1)}, f32[16,3]{1,0:T(8,128)}, u32[]{:S(2)}) %copy-start) | copy-done | bytes 216
  2.1 0.0 copy-done.1
  2.2 0.0 copy-done.2
  2.2 41.1 %shard_map.68 = (f32[4,3,768]{2,1,0:T(4,128)S(1)}, f32[4,3,768]{2,1,0:T(4,128)S(1)}) custom-call(f32[16,16]{1,0:T(8,128)S(1)} %copy-done.1, f32[16,3]{1,0:T(8,128)S(1)} %copy-done, f32[4,3,768]{2,1,0:T(4,128)S(1)} %copy.7.pos_ref, f32[4,3,768]{2,1,0:T(4,128)S(1)} %copy.8.vel_ref, f32[768]{0:T(1024)S(1)} %copy-done.2), custom_call_target="tpu_custom_call" | custom-call | tf_op jit(solution)/shard_map/pallas_call | solution.py:349
  43.3 0.6 %copy.9 = f32[4,3,768]{2,0,1:T(4,128)} copy(f32[4,3,768]{2,1,0:T(4,128)S(1)} %get-tuple-element.2) | data formatting | bytes 73728 | tf_op jit(solution)/shard_map/pallas_call | solution.py:349
  43.9 0.6 %copy.10 = f32[4,3,768]{2,0,1:T(4,128)} copy(f32[4,3,768]{2,1,0:T(4,128)S(1)} %get-tuple-element.3) | data formatting | bytes 73728 | tf_op jit(solution)/shard_map/pallas_call | solution.py:349
  (1 shorter events, 0.0 us)
Async XLA Ops:
  0.6 0.8 %copy-start.3 = (f32[4,3,768]{2,0,1:T(4,128)S(1)}, f32[4,3,768]{2,0,1:T(4,128)}, u32[]{:S(2)}) copy-start(f32[4,3,768]{2,0,1:T(4,128)} %param.6) | copy-start | bytes 110596
  1.4 0.7 %copy-start = (f32[16,3]{1,0:T(8,128)S(1)}, f32[16,3]{1,0:T(8,128)}, u32[]{:S(2)}) copy-start(f32[16,3]{1,0:T(8,128)} %constant.5.clone.step_ref) | copy-start | bytes 580
  1.5 0.7 %copy-start.1 = (f32[16,16]{1,0:T(8,128)S(1)}, f32[16,16]{1,0:T(8,128)}, u32[]{:S(2)}) copy-start(f32[16,16]{1,0:T(8,128)} %constant.4.clone.table_ref) | copy-start | bytes 3076
  1.5 0.7 %copy-start.2 = (f32[768]{0:T(1024)S(1)}, f32[768]{0:T(1024)}, u32[]{:S(2)}) copy-start(f32[768]{0:T(1024)} %charge_ref.1) | copy-start | bytes 9220

commit v8 on v7

--- a/solution.py
+++ b/solution.py
@@ -131,12 +131,17 @@
     return [functools.partial(piece, lane) for lane in range(0, count, LANES)]
 
 
-def far_piece(start, near_moment, weights, back):
-    rows = pl.ds(start, ROWS)
-    back[:, rows] = lax.dot_general(
-        near_moment[...], weights[rows], (((1,), (1,)), ((), ())),
-        preferred_element_type=jnp.float32,
-    )
+def far_pieces(start, near_moment, weights, back):
+    rows, count = pl.ds(start, ROWS), weights.shape[1] // 2
+
+    def piece(first):
+        part = lax.dot_general(
+            near_moment[...], weights[rows, first : first + count], (((1,), (1,)), ((), ())),
+            preferred_element_type=jnp.float32,
+        )
+        back[:, rows] = part if first == 0 else back[:, rows] + part
+
+    return [functools.partial(piece, first) for first in (0, count)]
 
 
 def force_of(pos, charge, sums):
@@ -214,8 +219,7 @@
         centres[b] = centre
         pos = scaled(pack, centre)
         near_ops[b] = near_operand(pos)
-        moment = moment_parts(pos, charge).astype(jnp.bfloat16)
-        near_moments[b] = jnp.concatenate((moment, moment), axis=1)
+        near_moments[b] = moment_parts(pos, charge).astype(jnp.bfloat16)
         sums[b] = jnp.zeros((32, tile[1]), jnp.float32)
 
     def prepare(step):
@@ -238,10 +242,8 @@
             b = first + i
             pieces = near_pieces(start, rights.at[b], weights.at[i], sums.at[b])
             if with_back:
-                one = functools.partial(
-                    far_piece, start, near_moments.at[b], weights.at[i], raw_backs.at[b]
-                )
-                pieces.insert(1, one)
+                ones = far_pieces(start, near_moments.at[b], weights.at[i], raw_backs.at[b])
+                pieces = [pieces[0], ones[0], pieces[1], ones[1], *pieces[2:]]
             return pieces
 
         for piece in before(0):
@@ -357,7 +359,7 @@
             pltpu.VMEM((beads, 8, count), jnp.float32),
             pltpu.VMEM((beads, 8, count), jnp.float32),
             pltpu.VMEM((beads, 48, count), jnp.bfloat16),
-            pltpu.VMEM((beads, 32, 2 * count), jnp.bfloat16),
+            pltpu.VMEM((beads, 32, count), jnp.bfloat16),
             pltpu.VMEM((beads, 32, count), jnp.float32),
             pltpu.VMEM((half + 1, beads, 8, count), jnp.float32),
             pltpu.VMEM((half + 1, beads, 8, count), jnp.float32),

time: 44.8 us -> 44.9 us (level)
  no operation moved by 1% of the time
where the time goes in v8:
time: 44.9 us; the launch traced here: 44.6 us
  Pallas kernels  41.2 us (92%)
  local copies, waits for them, and re-layouts  2.74 us (6%)
  between operations  0.69 us (2%)
    pallas_call x1, Pallas kernels, local(): pl.pallas_call(functools.partial(kernel, n_bead, n_dom), out_shape=(shape...  41.2 us
    unnamed x10, local copies, waits for them, and re-layouts  1.48 us
    pallas_call x2, local copies, waits for them, and re-layouts, local(): pl.pallas_call(functools.partial(kernel, n_bead, n_dom), out_shape=(shape...  1.25 us

profile of v8, /device:TPU:0, one launch (start us, length us, event | category | flops | bytes accessed | tf_op | source)
XLA Modules:
  0.0 44.6 jit_solution(9885111279195897194)
XLA Ops:
  0.6 0.0 copy-start.3
  0.6 0.8 %copy.7.pos_ref = f32[4,3,768]{2,1,0:T(4,128)S(1)} copy(f32[4,3,768]{2,0,1:T(4,128)} %param.5) | data formatting | bytes 73728 | tf_op args[0]
  1.4 0.0 copy-done.3
  1.4 0.0 copy-start
  1.5 0.0 copy-start.1
  1.5 0.0 copy-start.2
  1.5 0.6 %copy-done = f32[16,3]{1,0:T(8,128)S(1)} copy-done((f32[16,3]{1,0:T(8,128)S(1)}, f32[16,3]{1,0:T(8,128)}, u32[]{:S(2)}) %copy-start) | copy-done | bytes 216
  2.1 0.0 copy-done.1
  2.2 0.0 copy-done.2
  2.2 41.2 %shard_map.68 = (f32[4,3,768]{2,1,0:T(4,128)S(1)}, f32[4,3,768]{2,1,0:T(4,128)S(1)}) custom-call(f32[16,16]{1,0:T(8,128)S(1)} %copy-done.1, f32[16,3]{1,0:T(8,128)S(1)} %copy-done, f32[4,3,768]{2,1,0:T(4,128)S(1)} %copy.7.pos_ref, f32[4,3,768]{2,1,0:T(4,128)S(1)} %copy.8.vel_ref, f32[768]{0:T(1024)S(1)} %copy-done.2), custom_call_target="tpu_custom_call" | custom-call | tf_op jit(solution)/shard_map/pallas_call | solution.py:351
  43.4 0.6 %copy.9 = f32[4,3,768]{2,0,1:T(4,128)} copy(f32[4,3,768]{2,1,0:T(4,128)S(1)} %get-tuple-element.2) | data formatting | bytes 73728 | tf_op jit(solution)/shard_map/pallas_call | solution.py:351
  44.0 0.6 %copy.10 = f32[4,3,768]{2,0,1:T(4,128)} copy(f32[4,3,768]{2,1,0:T(4,128)S(1)} %get-tuple-element.3) | data formatting | bytes 73728 | tf_op jit(solution)/shard_map/pallas_call | solution.py:351
  (1 shorter events, 0.0 us)
Async XLA Ops:
  0.6 0.8 %copy-start.3 = (f32[4,3,768]{2,0,1:T(4,128)S(1)}, f32[4,3,768]{2,0,1:T(4,128)}, u32[]{:S(2)}) copy-start(f32[4,3,768]{2,0,1:T(4,128)} %param.6) | copy-start | bytes 110596
  1.4 0.7 %copy-start = (f32[16,3]{1,0:T(8,128)S(1)}, f32[16,3]{1,0:T(8,128)}, u32[]{:S(2)}) copy-start(f32[16,3]{1,0:T(8,128)} %constant.5.clone.step_ref) | copy-start | bytes 580
  1.5 0.7 %copy-start.1 = (f32[16,16]{1,0:T(8,128)S(1)}, f32[16,16]{1,0:T(8,128)}, u32[]{:S(2)}) copy-start(f32[16,16]{1,0:T(8,128)} %constant.4.clone.table_ref) | copy-start | bytes 3076
  1.5 0.7 %copy-start.2 = (f32[768]{0:T(1024)S(1)}, f32[768]{0:T(1024)}, u32[]{:S(2)}) copy-start(f32[768]{0:T(1024)} %charge_ref.1) | copy-start | bytes 9220
